TPU v7x, 32 devices: a whole 2x2x4 slice. The times are simulated.
32 devices in a mesh: gz: 4 (over x, core), xy: 8 (over z, y).
Axes of the slice: x: 2, y: 2, z: 4, core: 2. Of those that a mesh axis runs over, the one named last changes fastest.
Arguments:
- features: float32 [64, 16, 28, 256], P('gz', 'xy'), may hold values from -6 to 6
- block_mask: int32 [32, 8, 14], P('gz', 'xy'), may hold values 0 or 1
- near_kernel_weight: float32 [27, 256, 256], P(None, None, 'xy'), may hold values from -0.078125 to 0.078125
- far_kernel_weight: float32 [27, 256, 256], P(None, None, 'xy'), may hold values from -0.078125 to 0.078125
Outputs:
- section_out: float32 [64, 16, 28, 256], P('gz', 'xy')
All inputs are finite; a program needn't handle non-finite values. No bound on the sum of `block_mask` on one device may be relied on, other than what follows from the above.
Results may differ from a plain program's by a relative error of at most 0.00005.
Values sent between devices are 32-bit elements; how exact they have to be, the bound alone decides.
A program may use at most 128 MiB of HBM per device.

v0:
```python
import jax
import jax.numpy as jnp
from jax import lax
from jax.sharding import PartitionSpec as P

B = 2
NEAR_DILATION = 16
FAR_DILATION = 32


def from_behind(block, axis, distance):
    devices = range(lax.axis_size(axis))
    route = [(i - distance, i) for i in devices if i - distance in devices]
    return lax.ppermute(block, axis, route)


def stack_z(field, step):
    lower = from_behind(field, "gz", step)
    upper = from_behind(field, "gz", -step)
    return jnp.stack((lower, field, upper), 0)


def stack_x(field, step):
    lower = from_behind(field, "xy", step)
    upper = from_behind(field, "xy", -step)
    return jnp.stack((lower, field, upper), 0)


def neighbours(field, step_z, step_x):
    both = stack_x(stack_z(field, step_z), step_x)
    return [[both[col, row] for col in range(3)] for row in range(3)]


def dilated_result(field, weight, dilation):
    slab_z, slab_x, span_y, channels = field.shape
    grid = neighbours(field, dilation // slab_z, dilation // slab_x)
    windows = []
    for row in range(3):
        for col in range(3):
            padded = jnp.pad(grid[row][col], ((0, 0), (0, 0), (dilation, dilation), (0, 0)))
            for lane in range(3):
                windows.append(padded[:, :, lane * dilation : lane * dilation + span_y, :])
    columns = jnp.concatenate(windows, 3).reshape(slab_z * slab_x * span_y, 27 * channels)
    summed = jnp.dot(
        columns,
        weight.reshape(27 * channels, weight.shape[2]),
        precision=lax.Precision.HIGHEST,
        preferred_element_type=jnp.float32,
    )
    return summed.reshape(slab_z, slab_x, span_y, weight.shape[2])


def local(features, block_mask, near_kernel_weight, far_kernel_weight):
    active_blocks = jnp.repeat(jnp.repeat(jnp.repeat(block_mask, B, 0), B, 1), B, 2)
    active_blocks = active_blocks.astype(jnp.float32)[..., None]
    dense_near_output = lax.all_gather(near_kernel_weight, "xy", axis=2, tiled=True)
    masked_input = active_blocks * features
    hidden_state = active_blocks * jnp.maximum(
        dilated_result(masked_input, dense_near_output, NEAR_DILATION), 0.0
    )
    dense_far_output = lax.all_gather(far_kernel_weight, "xy", axis=2, tiled=True)
    return active_blocks * (
        masked_input + dilated_result(hidden_state, dense_far_output, FAR_DILATION)
    )


def solution(mesh):
    in_specs = (
        P("gz", "xy", None, None),
        P("gz", "xy", None),
        P(None, None, "xy"),
        P(None, None, "xy"),
    )
    out_specs = P("gz", "xy", None, None)
    return jax.shard_map(local, mesh=mesh, in_specs=in_specs, out_specs=out_specs, check_vma=False)
```

profile of v0, /device:TPU:1, one launch (start us, length us, event | category | flops | bytes accessed | tf_op | source)
XLA Modules:
  0.0 306.4 jit_solution(7012479819317506262)
XLA Ops:
  8.2 1.4 fusion.29
  10.2 2.0 collective-permute-start.1
  12.1 4.5 %collective-permute-start = (f32[16,2,28,256]{3,0,2,1:T(8,128)S(1)}, f32[16,2,28,256]{3,0,2,1:T(8,128)S(1)}, u32[]{:S(2)}, u32[]{:S(2)}) collective-permute-start(f32[16,2,28,256]{3,0,2,1:T(8,128)S(1)} %copy.28), channel_id=1, source_target_pairs={{0,8},{8,16},{16,24},{1,9},{9,17},{17,25},{2,10},{10,18},{18,26},{... | collective-permute-start | bytes 2752520 | tf_op jit(solution)/shard_map/ppermute | solution.py:14
  16.6 9.5 %collective-permute-done.1 = f32[16,2,28,256]{3,0,2,1:T(8,128)S(1)} collective-permute-done((f32[16,2,28,256]{3,0,2,1:T(8,128)S(1)}, f32[16,2,28,256]{3,0,2,1:T(8,128)S(1)}, u32[]{:S(2)}, u32[]{:S(2)}) %collective-permute-start.1) | collective-permute-done | bytes 917536 | tf_op jit(solution)/shard_map/ppermute | solution.py:14
  28.3 3.1 %copy.32 = f32[3,16,2,28,256]{4,1,3,2,0:T(8,128)} copy(f32[3,16,2,28,256]{4,3,2,1,0:T(8,128)S(1)} %get-tuple-element.14) | data formatting | bytes 5505024 | tf_op jit(solution)/shard_map/stack | solution.py:20
  31.4 2.2 collective-permute-start.2
  34.0 3.4 %copy.57 = f32[3,16,2,28,256]{4,3,2,1,0:T(8,128)S(1)} copy(f32[3,16,2,28,256]{4,1,3,2,0:T(8,128)} %collective-permute-done.2) | data formatting | bytes 5505024 | tf_op jit(solution)/shard_map/ppermute | solution.py:14
  37.9 1.2 fusion.17
  40.2 1.2 fusion.19
  41.4 1.2 fusion.2
  43.6 1.2 fusion.3
  44.9 1.2 fusion.18
  46.0 1.2 constant_dynamic-update-slice_fusion.6
  49.5 1.2 constant_dynamic-update-slice_fusion.5
  50.7 1.1 fusion.23
  51.8 1.2 fusion.4
  54.1 1.2 fusion.5
  57.5 1.2 fusion.24
  60.9 1.2 fusion.27
  62.1 1.1 fusion.6
  64.4 1.2 fusion.7
  65.6 1.2 fusion.26
  68.0 1.2 fusion.28
  69.1 50.9 %all-gather.3.cloned.1.call-done = f32[27,256,256]{1,2,0:T(8,128)} async-done(((f32[27,256,32]{1,2,0:T(8,128)}), f32[27,256,256]{1,2,0:T(8,128)}) %all-gather.3.cloned.1.call-update) | async-done | bytes 7077904 | tf_op jit(solution)/shard_map/all_gather | solution.py:56
  120.0 8.0 %copy.34 = f32[27,256,256]{2,1,0:T(8,128)} copy(f32[27,256,256]{1,2,0:T(8,128)} %all-gather.3.cloned.1.call-done) | data formatting | bytes 14155776 | tf_op jit(solution)/shard_map/all_gather | solution.py:56
  128.0 27.7 %fusion = f32[16,2,28,256]{3,2,1,0:T(8,128)S(1)} fusion(f32[16,2,28,6912]{3,2,1,0:T(8,128)} %fusion.28, f32[6912,256,1,1]{1,0,3,2:T(8,128)} %bitcast.121, f32[16,28]{1,0:T(8,128)S(1)} %copy.26), kind=kOutput, calls=%fused_computation.17 | convolution fusion | flops 19025821696 | bytes 32769792 | tf_op jit(solution)/shard_map/dot_general | solution.py:44
  156.3 1.3 collective-permute-start.4
  157.6 4.1 %collective-permute-start.3 = (f32[16,2,28,256]{3,0,2,1:T(8,128)S(1)}, f32[16,2,28,256]{3,0,2,1:T(8,128)S(1)}, u32[]{:S(2)}, u32[]{:S(2)}) collective-permute-start(f32[16,2,28,256]{3,0,2,1:T(8,128)S(1)} %copy.35), channel_id=1, source_target_pairs={{0,16},{8,24},{1,17},{9,25},{2,18},{10,26},{3,19},{11,27},{4,20},{... | collective-permute-start | bytes 2752520 | tf_op jit(solution)/shard_map/ppermute | solution.py:14
  161.7 17.6 %collective-permute-done.4 = f32[16,2,28,256]{3,0,2,1:T(8,128)S(1)} collective-permute-done((f32[16,2,28,256]{3,0,2,1:T(8,128)S(1)}, f32[16,2,28,256]{3,0,2,1:T(8,128)S(1)}, u32[]{:S(2)}, u32[]{:S(2)}) %collective-permute-start.4) | collective-permute-done | bytes 917536 | tf_op jit(solution)/shard_map/ppermute | solution.py:14
  181.4 3.1 %copy.39 = f32[3,16,2,28,256]{4,1,3,2,0:T(8,128)} copy(f32[3,16,2,28,256]{4,3,2,1,0:T(8,128)S(1)} %get-tuple-element.6) | data formatting | bytes 5505024 | tf_op jit(solution)/shard_map/stack | solution.py:20
  184.5 2.2 collective-permute-start.5
  187.8 41.4 %all-gather.5.cloned.1.call-done = f32[27,256,256]{1,2,0:T(8,128)} async-done(((f32[27,256,32]{1,2,0:T(8,128)}), f32[27,256,256]{1,2,0:T(8,128)}) %all-gather.5.cloned.1.call-update) | async-done | bytes 7077904 | tf_op jit(solution)/shard_map/all_gather | solution.py:61
  229.2 8.0 %copy.41 = f32[27,256,256]{2,1,0:T(8,128)} copy(f32[27,256,256]{1,2,0:T(8,128)} %all-gather.5.cloned.1.call-done) | data formatting | bytes 14155776 | tf_op jit(solution)/shard_map/all_gather | solution.py:61
  237.2 3.5 %copy.56 = f32[3,16,2,28,256]{4,3,2,1,0:T(8,128)S(1)} copy(f32[3,16,2,28,256]{4,1,3,2,0:T(8,128)} %collective-permute-done.5) | data formatting | bytes 5505024 | tf_op jit(solution)/shard_map/ppermute | solution.py:14
  241.9 1.2 broadcast_dynamic-update-slice_fusion.15
  243.1 1.2 broadcast_dynamic-update-slice_fusion.14
  245.4 1.2 broadcast_dynamic-update-slice_fusion.13
  246.6 1.1 broadcast_dynamic-update-slice_fusion.12
  247.7 1.2 fusion.12
  251.2 1.2 fusion.13
  253.5 1.1 broadcast_dynamic-update-slice_fusion.8
  255.7 1.2 broadcast_dynamic-update-slice_fusion.7
  262.5 1.2 broadcast_dynamic-update-slice_fusion.3
  265.9 1.2 broadcast_dynamic-update-slice_fusion.1
  267.1 1.2 broadcast_dynamic-update-slice_fusion
  269.5 1.2 broadcast_dynamic-update-slice_fusion.17
  270.7 27.3 %fusion.1 = f32[16,2,28,256]{3,2,1,0:T(8,128)S(1)} fusion(f32[16,2,28,6912]{3,2,1,0:T(8,128)} %broadcast_dynamic-update-slice_fusion.17, f32[6912,256,1,1]{1,0,3,2:T(8,128)S(1)} %bitcast.114, f32[16,28]{1,0:T(8,128)S(1)} %copy.26, f32[16,2,28,256]{3,1,2,0:T(2,128)S(1)} %copy-done), kind=kOutput, calls=%fused_computation.19 | convolution fusion | flops 19026051072 | bytes 33687296 | tf_op jit(solution)/shard_map/dot_general | solution.py:44
  297.9 1.6 copy.42
  (57 shorter events, 36.9 us)
Async XLA Ops:
  6.5 113.5 %all-gather.3.cloned.1.call-start = ((), (), s32[]{:S(2)}) async-start(), calls=%async_computation | async-start | bytes 7962624 | tf_op jit(solution)/shard_map/all_gather | solution.py:56
  7.3 222.0 %all-gather.5.cloned.1.call-start = ((), (), s32[]{:S(2)}) async-start(), calls=%async_computation.1 | async-start | bytes 7962624 | tf_op jit(solution)/shard_map/all_gather | solution.py:61
  10.2 16.0 %collective-permute-start.1 = (f32[16,2,28,256]{3,0,2,1:T(8,128)S(1)}, f32[16,2,28,256]{3,0,2,1:T(8,128)S(1)}, u32[]{:S(2)}, u32[]{:S(2)}) collective-permute-start(f32[16,2,28,256]{3,0,2,1:T(8,128)S(1)} %copy.28), channel_id=1, source_target_pairs={{8,0},{16,8},{24,16},{9,1},{17,9},{25,17},{10,2},{18,10},{26,18},{... | collective-permute-start | bytes 2752520 | tf_op jit(solution)/shard_map/ppermute | solution.py:14
  12.1 14.8 %collective-permute-start = (f32[16,2,28,256]{3,0,2,1:T(8,128)S(1)}, f32[16,2,28,256]{3,0,2,1:T(8,128)S(1)}, u32[]{:S(2)}, u32[]{:S(2)}) collective-permute-start(f32[16,2,28,256]{3,0,2,1:T(8,128)S(1)} %copy.28), channel_id=1, source_target_pairs={{0,8},{8,16},{16,24},{1,9},{9,17},{17,25},{2,10},{10,18},{18,26},{... | collective-permute-start | bytes 2752520 | tf_op jit(solution)/shard_map/ppermute | solution.py:14
  31.4 2.6 collective-permute-start.2
  156.3 23.0 %collective-permute-start.4 = (f32[16,2,28,256]{3,0,2,1:T(8,128)S(1)}, f32[16,2,28,256]{3,0,2,1:T(8,128)S(1)}, u32[]{:S(2)}, u32[]{:S(2)}) collective-permute-start(f32[16,2,28,256]{3,0,2,1:T(8,128)S(1)} %copy.35), channel_id=1, source_target_pairs={{16,0},{24,8},{17,1},{25,9},{18,2},{26,10},{19,3},{27,11},{20,4},{... | collective-permute-start | bytes 2752520 | tf_op jit(solution)/shard_map/ppermute | solution.py:14
  157.6 22.5 %collective-permute-start.3 = (f32[16,2,28,256]{3,0,2,1:T(8,128)S(1)}, f32[16,2,28,256]{3,0,2,1:T(8,128)S(1)}, u32[]{:S(2)}, u32[]{:S(2)}) collective-permute-start(f32[16,2,28,256]{3,0,2,1:T(8,128)S(1)} %copy.35), channel_id=1, source_target_pairs={{0,16},{8,24},{1,17},{9,25},{2,18},{10,26},{3,19},{11,27},{4,20},{... | collective-permute-start | bytes 2752520 | tf_op jit(solution)/shard_map/ppermute | solution.py:14
  184.5 52.8 %collective-permute-start.5 = (f32[3,16,2,28,256]{4,1,3,2,0:T(8,128)}, f32[3,16,2,28,256]{4,1,3,2,0:T(8,128)}, u32[]{:S(2)}, u32[]{:S(2)}) collective-permute-start(f32[3,16,2,28,256]{4,1,3,2,0:T(8,128)} %copy.39), channel_id=1, source_target_pairs={} | collective-permute-start | bytes 8257544 | tf_op jit(solution)/shard_map/ppermute | solution.py:14
  237.2 33.4 %slice-start = ((s8[7077888]{0:T(1024)(128)(4,1)}), s8[4194304]{0:T(1024)(128)(4,1)S(1)}, s32[]{:S(2)}) async-start(s8[7077888]{0:T(1024)(128)(4,1)} %bitcast.112), calls=%async_computation.2 | async-start | bytes 8388608
  237.2 33.4 %copy-start = (f32[16,2,28,256]{3,1,2,0:T(2,128)S(1)}, f32[16,2,28,256]{3,1,2,0:T(2,128)}, u32[]{:S(2)}) copy-start(f32[16,2,28,256]{3,1,2,0:T(2,128)} %param.4) | copy-start | bytes 2752516
  252.3 18.3 %slice-start.1 = ((s8[7077888]{0:T(1024)(128)(4,1)}), s8[2883584]{0:T(1024)(128)(4,1)S(1)}, s32[]{:S(2)}) async-start(s8[7077888]{0:T(1024)(128)(4,1)} %bitcast.112), calls=%async_computation.3 | async-start | bytes 5767168
Sparse Core Ops, SparseCore 0:
  9.5 110.4 all-gather.2
  122.2 106.9 all-gather.4
where the time goes:
time: 308 us; the launch traced here: 306 us
  waiting for transfers between devices  121 us (39%)
  local copies, waits for them, and re-layouts  97.2 us (32%)
  matrix products  55 us (18%)
  starting transfers between devices  16.3 us (5%)
  between operations  13.6 us (4%)
  other arithmetic  3.6 us (1%)
    unnamed x58, local copies, waits for them, and re-layouts  59.9 us
    dot_general x2, matrix products, dilated_result(): jnp.dot(columns, weight.reshape(27 * channels, weight.shape[2]), precisio...  55 us
    all_gather x1, waiting for transfers between devices, local(): lax.all_gather(near_kernel_weight, 'xy', axis=2, tiled=True)  50.9 us
    all_gather x1, waiting for transfers between devices, local(): lax.all_gather(far_kernel_weight, 'xy', axis=2, tiled=True)  41.4 us
    ppermute x6, waiting for transfers between devices, from_behind(): return lax.ppermute(block, axis, route)  27.7 us
    ppermute x6, starting transfers between devices, from_behind(): return lax.ppermute(block, axis, route)  16.3 us
    ppermute x6, local copies, waits for them, and re-layouts, from_behind(): return lax.ppermute(block, axis, route)  9.13 us
    all_gather x1, local copies, waits for them, and re-layouts, local(): lax.all_gather(near_kernel_weight, 'xy', axis=2, tiled=True)  7.97 us
  transfers between devices with their start and end apart: 8, of which 6 were waited for; matrix products, arithmetic and copies ran while one was open for 31% of the time, Pallas kernels for 0%

commit v1 on v0

v1 whole, which is shorter than its diff:
```python
import jax
import jax.numpy as jnp
from jax import lax
from jax.sharding import PartitionSpec as P

B = 2
NEAR_DILATION = 16
FAR_DILATION = 32


def offsets(dilation, extent):
    return (-1, 0, 1) if dilation < extent else (0,)


def from_behind(block, axis, distance):
    if distance == 0:
        return block
    devices = range(lax.axis_size(axis))
    route = [(i - distance, i) for i in devices if i - distance in devices]
    return lax.ppermute(block, axis, route)


def reach(field, dilation):
    slab_z, slab_x, span_y, _ = field.shape
    return (
        offsets(dilation, slab_z * lax.axis_size("gz")),
        offsets(dilation, slab_x * lax.axis_size("xy")),
        offsets(dilation, span_y),
    )


def gathered(weight, taps):
    cube = weight.reshape((3, 3, 3) + weight.shape[1:])
    for dim, tap in enumerate(taps):
        cube = cube if len(tap) == 3 else lax.slice_in_dim(cube, 1, 2, axis=dim)
    flat = cube.reshape((-1,) + weight.shape[1:])
    return lax.all_gather(flat, "xy", axis=2, tiled=True)


def dilated_result(field, weight, taps, dilation):
    slab_z, slab_x, span_y, channels = field.shape
    windows = []
    for a in taps[0]:
        over_z = from_behind(field, "gz", -a * dilation // slab_z)
        for b in taps[1]:
            over_x = from_behind(over_z, "xy", -b * dilation // slab_x)
            for c in taps[2]:
                if c == 0:
                    windows.append(over_x)
                elif c < 0:
                    part = over_x[:, :, : span_y - dilation]
                    windows.append(jnp.pad(part, ((0, 0), (0, 0), (dilation, 0), (0, 0))))
                else:
                    part = over_x[:, :, dilation:]
                    windows.append(jnp.pad(part, ((0, 0), (0, 0), (0, dilation), (0, 0))))
    columns = jnp.concatenate(windows, 3).reshape(slab_z * slab_x * span_y, -1)
    summed = jnp.dot(
        columns,
        weight.reshape(-1, weight.shape[2]),
        precision=lax.Precision.HIGH,
        preferred_element_type=jnp.float32,
    )
    return summed.reshape(slab_z, slab_x, span_y, weight.shape[2])


def local(features, block_mask, near_kernel_weight, far_kernel_weight):
    near_taps = reach(features, NEAR_DILATION)
    far_taps = reach(features, FAR_DILATION)
    active = jnp.repeat(jnp.repeat(jnp.repeat(block_mask, B, 0), B, 1), B, 2)
    active = active.astype(jnp.float32)[..., None]
    near_weight = gathered(near_kernel_weight, near_taps)
    far_weight = gathered(far_kernel_weight, far_taps)
    masked = active * features
    hidden = active * jnp.maximum(
        dilated_result(masked, near_weight, near_taps, NEAR_DILATION), 0.0
    )
    return active * (masked + dilated_result(hidden, far_weight, far_taps, FAR_DILATION))


def solution(mesh):
    in_specs = (
        P("gz", "xy", None, None),
        P("gz", "xy", None),
        P(None, None, "xy"),
        P(None, None, "xy"),
    )
    out_specs = P("gz", "xy", None, None)
    return jax.shard_map(local, mesh=mesh, in_specs=in_specs, out_specs=out_specs, check_vma=False)
```

time: 308 us -> 129 us (0.42)
  the two profiles are of different devices: /device:TPU:1 before, /device:TPU:2 now
where the time goes in v1:
time: 129 us
  waiting for transfers between devices  33.8 us (26%)
  blocking collectives  32.4 us (25%)
  local copies, waits for them, and re-layouts  23 us (18%)
  between operations  13.5 us (10%)
  starting transfers between devices  13.3 us (10%)
  matrix products  9.63 us (7%)
  other arithmetic  3.23 us (3%)
    all_gather x1, blocking collectives, gathered(): return lax.all_gather(flat, 'xy', axis=2, tiled=True)  32.4 us
    all_gather x1, waiting for transfers between devices, gathered(): return lax.all_gather(flat, 'xy', axis=2, tiled=True)  23.5 us
    ppermute x4, starting transfers between devices, from_behind(): return lax.ppermute(block, axis, route)  13.3 us
    ppermute x4, waiting for transfers between devices, from_behind(): return lax.ppermute(block, axis, route)  10.3 us
    unnamed x13, local copies, waits for them, and re-layouts  9.85 us
    dot_general x2, matrix products, dilated_result(): jnp.dot(columns, weight.reshape(-1, weight.shape[2]), precision=lax.Preci...  9.63 us
    ppermute x2, local copies, waits for them, and re-layouts, from_behind(): return lax.ppermute(block, axis, route)  3.45 us
    all_gather x2, local copies, waits for them, and re-layouts, gathered(): return lax.all_gather(flat, 'xy', axis=2, tiled=True)  2.75 us
  transfers between devices with their start and end apart: 5, of which 3 were waited for; matrix products, arithmetic and copies ran while one was open for 14% of the time, Pallas kernels for 0%

profile of v1, /device:TPU:2, one launch (start us, length us, event | category | flops | bytes accessed | tf_op | source)
XLA Modules:
  0.0 128.9 jit_solution(6869820628914423248)
XLA Ops:
  6.5 0.0 all-gather.3.cloned.1.call-start
  6.5 1.7 %slice.40 = f32[3,1,3,256,32]{3,4,2,1,0:T(8,128)} slice(f32[3,3,3,256,32]{3,4,2,1,0:T(8,128)} %bitcast.27), slice={[0:3], [1:2], [0:3], [0:256], [0:32]} | slice | bytes 589824 | tf_op jit(solution)/shard_map/slice | solution.py:35
  8.2 0.0 all-gather.3.cloned.1.call-update
  8.3 0.7 convert_bitcast_fusion
  9.0 0.1 copy.46
  9.1 0.1 copy.47
  9.1 0.0 copy-start
  9.2 1.4 %copy_multiply_fusion = f32[16,2,28,256]{3,2,1,0:T(8,128)S(1)} fusion(f32[16,2,28,256]{3,1,2,0:T(2,128)} %param.4, f32[16,28]{1,0:T(8,128)S(1)} %copy.47), kind=kLoop, calls=%fused_computation.10 | loop fusion | flops 229376 | bytes 1836800 | tf_op jit(solution)/shard_map/mul | solution.py:73
  10.6 0.5 copy.49
  11.1 1.9 %collective-permute-start = (f32[16,2,28,256]{3,0,2,1:T(8,128)S(1)}, f32[16,2,28,256]{3,0,2,1:T(8,128)S(1)}, u32[]{:S(2)}, u32[]{:S(2)}) collective-permute-start(f32[16,2,28,256]{3,0,2,1:T(8,128)S(1)} %copy.49), channel_id=1, source_target_pairs={{0,8},{8,16},{16,24},{1,9},{9,17},{17,25},{2,10},{10,18},{18,26},{... | collective-permute-start | bytes 2752520 | tf_op jit(solution)/shard_map/ppermute | solution.py:20
  13.0 3.6 %collective-permute-start.1 = (f32[16,2,28,256]{3,0,2,1:T(8,128)S(1)}, f32[16,2,28,256]{3,0,2,1:T(8,128)S(1)}, u32[]{:S(2)}, u32[]{:S(2)}) collective-permute-start(f32[16,2,28,256]{3,0,2,1:T(8,128)S(1)} %copy.49), channel_id=1, source_target_pairs={{8,0},{16,8},{24,16},{9,1},{17,9},{25,17},{10,2},{18,10},{26,18},{... | collective-permute-start | bytes 2752520 | tf_op jit(solution)/shard_map/ppermute | solution.py:20
  16.7 0.1 fusion.14
  16.8 9.0 %collective-permute-done = f32[16,2,28,256]{3,0,2,1:T(8,128)S(1)} collective-permute-done((f32[16,2,28,256]{3,0,2,1:T(8,128)S(1)}, f32[16,2,28,256]{3,0,2,1:T(8,128)S(1)}, u32[]{:S(2)}, u32[]{:S(2)}) %collective-permute-start) | collective-permute-done | bytes 917536 | tf_op jit(solution)/shard_map/ppermute | solution.py:20
  25.8 0.1 fusion.16
  25.9 0.2 copy.76
  26.1 0.2 copy.77
  26.4 1.2 collective-permute-done.1
  27.6 0.1 fusion.15
  27.6 0.2 copy.78
  27.9 0.2 copy.79
  28.1 1.2 pad_dynamic-update-slice_fusion.5
  29.3 1.6 %constant_dynamic-update-slice_fusion.2 = f32[16,2,28,2304]{3,2,1,0:T(8,128)} fusion(f32[16,2,28,2304]{3,2,1,0:T(8,128)} %pad_dynamic-update-slice_fusion.5, f32[16,2,28,256]{3,0,2,1:T(8,128)S(1)} %collective-permute-done), kind=kLoop, calls=%fused_computation.19 | loop fusion | bytes 1966080
  30.9 1.1 pad_dynamic-update-slice_fusion.4
  32.0 1.1 pad_dynamic-update-slice_fusion.3
  33.2 0.0 copy-done
  33.2 1.1 constant_dynamic-update-slice_fusion.1
  34.3 1.1 pad_dynamic-update-slice_fusion.2
  35.4 1.2 pad_dynamic-update-slice_fusion.1
  36.6 1.5 %constant_dynamic-update-slice_fusion = f32[16,2,28,2304]{3,2,1,0:T(8,128)} fusion(f32[16,2,28,2304]{3,2,1,0:T(8,128)} %pad_dynamic-update-slice_fusion.1, f32[16,2,28,256]{3,0,2,1:T(8,128)S(1)} %collective-permute-done.1), kind=kLoop, calls=%fused_computation.17 | loop fusion | bytes 1966080
  38.1 1.2 pad_dynamic-update-slice_fusion
  39.3 23.5 %all-gather.3.cloned.1.call-done = f32[9,256,256]{1,2,0:T(8,128)} async-done(((f32[9,256,32]{1,2,0:T(8,128)}), f32[9,256,256]{1,2,0:T(8,128)}) %all-gather.3.cloned.1.call-update) | async-done | bytes 2359312 | tf_op jit(solution)/shard_map/all_gather | solution.py:37
  62.9 2.0 %copy.58 = f32[9,256,256]{2,1,0:T(8,128)S(1)} copy(f32[9,256,256]{1,2,0:T(8,128)} %all-gather.3.cloned.1.call-done) | data formatting | bytes 4718592 | tf_op jit(solution)/shard_map/all_gather | solution.py:37
  64.9 7.0 %fusion.6 = f32[16,2,28,256]{3,2,1,0:T(8,128)S(1)} fusion(f32[16,2,28,2304]{3,2,1,0:T(8,128)} %pad_dynamic-update-slice_fusion, f32[2304,256,1,1]{1,0,3,2:T(8,128)S(1)} %bitcast.24, f32[16,28]{1,0:T(8,128)S(1)} %copy.47), kind=kOutput, calls=%fused_computation.7 | convolution fusion | flops 3171352576 | bytes 11536128 | tf_op jit(solution)/shard_map/dot_general | solution.py:57
  71.9 0.5 copy.59
  72.5 1.3 %collective-permute-start.2 = (f32[16,2,28,256]{3,0,2,1:T(8,128)S(1)}, f32[16,2,28,256]{3,0,2,1:T(8,128)}, u32[]{:S(2)}, u32[]{:S(2)}) collective-permute-start(f32[16,2,28,256]{3,0,2,1:T(8,128)S(1)} %copy.59), channel_id=1, source_target_pairs={{0,16},{8,24},{1,17},{9,25},{2,18},{10,26},{3,19},{11,27},{4,20},{... | collective-permute-start | bytes 2752520 | tf_op jit(solution)/shard_map/ppermute | solution.py:20
  73.8 6.5 %collective-permute-start.3 = (f32[16,2,28,256]{3,0,2,1:T(8,128)S(1)}, f32[16,2,28,256]{3,0,2,1:T(8,128)}, u32[]{:S(2)}, u32[]{:S(2)}) collective-permute-start(f32[16,2,28,256]{3,0,2,1:T(8,128)S(1)} %copy.59), channel_id=1, source_target_pairs={{16,0},{24,8},{17,1},{25,9},{18,2},{26,10},{19,3},{27,11},{20,4},{... | collective-permute-start | bytes 2752520 | tf_op jit(solution)/shard_map/ppermute | solution.py:20
  80.2 0.9 slice.41
  81.1 0.1 copy.63
  81.2 32.4 %all-gather = f32[3,1,1,256,256]{3,2,1,0,4:T(1,128)S(1)} all-gather(f32[3,1,1,256,32]{3,2,1,0,4:T(1,128)S(1)} %copy.63), channel_id=2, replica_groups=mesh['gz'=4,'xy'=8] {'xy'}, dimensions={4}, use_global_device_ids=true | all-gather | bytes 884736 | tf_op jit(solution)/shard_map/all_gather | solution.py:37
  113.6 0.7 copy.64
  114.3 0.0 collective-permute-done.2
  114.4 1.7 %copy.61 = f32[16,2,28,256]{3,2,1,0:T(8,128)S(1)} copy(f32[16,2,28,256]{3,0,2,1:T(8,128)} %collective-permute-done.2) | data formatting | bytes 1835008 | tf_op jit(solution)/shard_map/ppermute | solution.py:20
  116.1 0.0 collective-permute-done.3
  116.1 1.7 %copy.62 = f32[16,2,28,256]{3,2,1,0:T(8,128)S(1)} copy(f32[16,2,28,256]{3,0,2,1:T(8,128)} %collective-permute-done.3) | data formatting | bytes 1835008 | tf_op jit(solution)/shard_map/ppermute | solution.py:20
  117.8 2.6 %fusion.10 = f32[16,2,28,256]{3,2,1,0:T(8,128)S(1)} fusion(f32[768,256,1,1]{1,0,3,2:T(8,128)S(1)} %bitcast.25, f32[16,2,28,256]{3,2,1,0:T(8,128)S(1)} %copy.62, f32[16,2,28,256]{3,2,1,0:T(8,128)S(1)} %fusion.6, f32[16,2,28,256]{3,2,1,0:T(8,128)S(1)} %copy.61, f32[16,28]{1,0:T(8,128)S(1)} %copy.47, f32[16,2,28,256]{3,1,2,0:T(2,128)} %param.4), kind=kOutput, calls=%fused_computation.9 | convolution fusion | flops 1059028992 | bytes 5375744 | tf_op jit(solution)/shard_map/dot_general | solution.py:57
  120.4 1.6 %copy.65 = f32[16,2,28,256]{3,1,2,0:T(2,128)} copy(f32[16,2,28,256]{3,2,1,0:T(8,128)S(1)} %fusion.10) | data formatting | bytes 1835008 | tf_op jit(solution)/shard_map/mul | solution.py:77
  (3 shorter events, 0.0 us)
Async XLA Ops:
  6.5 56.4 %all-gather.3.cloned.1.call-start = ((), (), s32[]{:S(2)}) async-start(), calls=%async_computation | async-start | bytes 2654208 | tf_op jit(solution)/shard_map/all_gather | solution.py:37
  9.1 24.0 %copy-start = (f32[16,2,28,256]{3,1,2,0:T(2,128)S(1)}, f32[16,2,28,256]{3,1,2,0:T(2,128)}, u32[]{:S(2)}) copy-start(f32[16,2,28,256]{3,1,2,0:T(2,128)} %param.4) | copy-start | bytes 2752516
  11.1 14.7 %collective-permute-start = (f32[16,2,28,256]{3,0,2,1:T(8,128)S(1)}, f32[16,2,28,256]{3,0,2,1:T(8,128)S(1)}, u32[]{:S(2)}, u32[]{:S(2)}) collective-permute-start(f32[16,2,28,256]{3,0,2,1:T(8,128)S(1)} %copy.49), channel_id=1, source_target_pairs={{0,8},{8,16},{16,24},{1,9},{9,17},{17,25},{2,10},{10,18},{18,26},{... | collective-permute-start | bytes 2752520 | tf_op jit(solution)/shard_map/ppermute | solution.py:20
  13.0 14.5 %collective-permute-start.1 = (f32[16,2,28,256]{3,0,2,1:T(8,128)S(1)}, f32[16,2,28,256]{3,0,2,1:T(8,128)S(1)}, u32[]{:S(2)}, u32[]{:S(2)}) collective-permute-start(f32[16,2,28,256]{3,0,2,1:T(8,128)S(1)} %copy.49), channel_id=1, source_target_pairs={{8,0},{16,8},{24,16},{9,1},{17,9},{25,17},{10,2},{18,10},{26,18},{... | collective-permute-start | bytes 2752520 | tf_op jit(solution)/shard_map/ppermute | solution.py:20
  72.5 41.9 %collective-permute-start.2 = (f32[16,2,28,256]{3,0,2,1:T(8,128)S(1)}, f32[16,2,28,256]{3,0,2,1:T(8,128)}, u32[]{:S(2)}, u32[]{:S(2)}) collective-permute-start(f32[16,2,28,256]{3,0,2,1:T(8,128)S(1)} %copy.59), channel_id=1, source_target_pairs={{0,16},{8,24},{1,17},{9,25},{2,18},{10,26},{3,19},{11,27},{4,20},{... | collective-permute-start | bytes 2752520 | tf_op jit(solution)/shard_map/ppermute | solution.py:20
  73.8 42.3 %collective-permute-start.3 = (f32[16,2,28,256]{3,0,2,1:T(8,128)S(1)}, f32[16,2,28,256]{3,0,2,1:T(8,128)}, u32[]{:S(2)}, u32[]{:S(2)}) collective-permute-start(f32[16,2,28,256]{3,0,2,1:T(8,128)S(1)} %copy.59), channel_id=1, source_target_pairs={{16,0},{24,8},{17,1},{25,9},{18,2},{26,10},{19,3},{27,11},{20,4},{... | collective-permute-start | bytes 2752520 | tf_op jit(solution)/shard_map/ppermute | solution.py:20
Sparse Core Ops, SparseCore 0:
  9.5 53.2 all-gather.2

commit v2 on v1

--- a/solution.py
+++ b/solution.py
@@ -1,11 +1,17 @@
+import functools
+
 import jax
 import jax.numpy as jnp
 from jax import lax
+from jax.experimental import pallas as pl
+from jax.experimental.pallas import tpu as pltpu
 from jax.sharding import PartitionSpec as P
 
 B = 2
 NEAR_DILATION = 16
 FAR_DILATION = 32
+MESH = pl.DeviceIdType.MESH
+GROUP = 2
 
 
 def offsets(dilation, extent):
@@ -63,7 +69,7 @@
     return summed.reshape(slab_z, slab_x, span_y, weight.shape[2])
 
 
-def local(features, block_mask, near_kernel_weight, far_kernel_weight):
+def general(features, block_mask, near_kernel_weight, far_kernel_weight):
     near_taps = reach(features, NEAR_DILATION)
     far_taps = reach(features, FAR_DILATION)
     active = jnp.repeat(jnp.repeat(jnp.repeat(block_mask, B, 0), B, 1), B, 2)
@@ -77,6 +83,359 @@
     return active * (masked + dilated_result(hidden, far_weight, far_taps, FAR_DILATION))
 
 
+def section_kernel(
+    n, deep, span_y, near_step, far_step,
+    feat, mask, near, far, out,
+    wall, stage, xs, ms, mf, xc, xl, xh, acc, hc,
+    up_send, down_send, pair_send, core_send, line_recv, pair_recv, core_recv,
+    x_send, x_recv, m_send, m_recv, r_send, r_recv, load_sem, own_sem,
+):
+    taps, wide, channels = wall.shape
+    part = near.shape[1]
+    half = part // 2
+    positions = wide // part
+    line = positions // 2
+    groups = taps // GROUP
+    rows = xs.shape[1]
+    plane = rows // deep
+    skip = plane * NEAR_DILATION // span_y
+    edge = plane - skip
+    side = deep * edge
+    near_taps = 9
+
+    g = lax.axis_index("gz")
+    s = lax.axis_index("xy")
+    pos, col = s // 2, s % 2
+    core = g % 2
+    twin = g + 1 - 2 * core
+    mate = s + 1 - 2 * col
+
+    home = pl.ds(pl.multiple_of(s * part, part), part)
+    loads = []
+    for a in range(3):
+        loads.append((near.at[pl.ds(9 * a + 3, 3)], wall.at[pl.ds(3 * a, 3), home, :]))
+    for a in range(3):
+        loads.append((far.at[pl.ds(9 * a + 4, 1)], wall.at[pl.ds(near_taps + a, 1), home, :]))
+    loads.append((feat.at[g], xs.at[g]))
+    loads = [pltpu.make_async_copy(a, b, load_sem.at[i]) for i, (a, b) in enumerate(loads)]
+    for load in loads:
+        load.start()
+
+    barrier = pltpu.get_barrier_semaphore()
+    for i in range(1, n):
+        pl.semaphore_signal(barrier, inc=1, device_id={"gz": (g + i) % n}, device_id_type=MESH)
+    pl.semaphore_signal(barrier, inc=1, device_id={"xy": mate}, device_id_type=MESH)
+
+    @pl.when(pos > 0)
+    def _():
+        pl.semaphore_signal(barrier, inc=1, device_id={"xy": s - 2}, device_id_type=MESH)
+
+    @pl.when(pos < line - 1)
+    def _():
+        pl.semaphore_signal(barrier, inc=1, device_id={"xy": s + 2}, device_id_type=MESH)
+
+    ms[g] = mask[g]
+    for load in loads:
+        load.wait()
+
+    @pl.when((pos > 0) & (pos < line - 1))
+    def _():
+        pl.semaphore_wait(barrier, n + 2)
+
+    @pl.when((pos == 0) | (pos == line - 1))
+    def _():
+        pl.semaphore_wait(barrier, n + 1)
+
+    def piece(p, q, h, grp):
+        start = pl.multiple_of((2 * p + q) * part + h * half, half)
+        return wall.at[pl.ds(GROUP * grp, GROUP), pl.ds(start, half), :]
+
+    def up(p, grp):
+        ref = piece(p, col, core, grp)
+        return pltpu.make_async_remote_copy(
+            ref, ref, up_send.at[p, grp], line_recv.at[p, grp], device_id={"xy": s + 2}, device_id_type=MESH)
+
+    def down(p, grp):
+        ref = piece(p, col, core, grp)
+        return pltpu.make_async_remote_copy(
+            ref, ref, down_send.at[p, grp], line_recv.at[p, grp], device_id={"xy": s - 2}, device_id_type=MESH)
+
+    def across(p, q, grp):
+        ref = piece(p, q, core, grp)
+        return pltpu.make_async_remote_copy(
+            ref, ref, pair_send.at[p, grp], pair_recv.at[p, grp], device_id={"xy": mate}, device_id_type=MESH)
+
+    def to_twin(p, q, h, grp):
+        ref = piece(p, q, h, grp)
+        where = 2 * p + q
+        return pltpu.make_async_remote_copy(
+            ref, ref, core_send.at[where, grp], core_recv.at[where, grp], device_id={"gz": twin}, device_id_type=MESH)
+
+    def both(t, act):
+        @pl.when(pos - t >= 0)
+        def _():
+            act(pos - t)
+
+        if t > 0:
+            @pl.when(pos + t < line)
+            def _():
+                act(pos + t)
+
+    def line_stage(t, grp):
+        @pl.when(pos - t >= 0)
+        def _():
+            if t > 0:
+                up(pos - t, grp).wait_recv()
+
+            @pl.when(pos + 1 < line)
+            def _():
+                up(pos - t, grp).start()
+
+            across(pos - t, col, grp).start()
+            if t > 0:
+                to_twin(pos - t, col, core, grp).start()
+
+        @pl.when(pos + t < line)
+        def _():
+            if t > 0:
+                down(pos + t, grp).wait_recv()
+
+            @pl.when(pos >= 1)
+            def _():
+                down(pos + t, grp).start()
+
+            if t > 0:
+                across(pos + t, col, grp).start()
+                to_twin(pos + t, col, core, grp).start()
+
+    def pair_stage(t, grp):
+        def act(p):
+            across(p, 1 - col, grp).wait_recv()
+            to_twin(p, 1 - col, core, grp).start()
+
+        both(t, act)
+
+    def core_stage(t, grp):
+        def act(p):
+            if t > 0:
+                to_twin(p, col, 1 - core, grp).wait_recv()
+            to_twin(p, 1 - col, 1 - core, grp).wait_recv()
+
+        both(t, act)
+
+    def finish(t, grp):
+        @pl.when(pos - t >= 0)
+        def _():
+            @pl.when(pos + 1 < line)
+            def _():
+                up(pos - t, grp).wait_send()
+
+            across(pos - t, col, grp).wait_send()
+            to_twin(pos - t, 1 - col, core, grp).wait_send()
+            if t > 0:
+                to_twin(pos - t, col, core, grp).wait_send()
+
+        @pl.when(pos + t < line)
+        def _():
+            @pl.when(pos >= 1)
+            def _():
+                down(pos + t, grp).wait_send()
+
+            if t > 0:
+                across(pos + t, col, grp).wait_send()
+                to_twin(pos + t, 1 - col, core, grp).wait_send()
+                to_twin(pos + t, col, core, grp).wait_send()
+
+    def exchange(src, dst, send, recv, d):
+        return pltpu.make_async_remote_copy(
+            src.at[d], dst.at[g], send.at[d], recv.at[g], device_id={"gz": d}, device_id_type=MESH)
+
+    def arrival(dst, send, recv, d):
+        return pltpu.make_async_remote_copy(
+            dst.at[d], dst.at[d], send.at[d], recv.at[d], device_id={"gz": d}, device_id_type=MESH)
+
+    def split(value, ref, start, count):
+        high = value.astype(jnp.bfloat16)
+        low = (value - high.astype(jnp.float32)).astype(jnp.bfloat16)
+        at = pl.ds(start, count)
+        ref[at, 0:channels] = high
+        ref[at, channels : 2 * channels] = low
+        ref[at, 2 * channels :] = high
+
+    def tap_weight(tap):
+        value = wall[tap]
+        high = value.astype(jnp.bfloat16)
+        low = (value - high.astype(jnp.float32)).astype(jnp.bfloat16)
+        return jnp.concatenate([high, high, low], axis=1)
+
+    def product(lhs, weight):
+        return lax.dot_general(lhs, weight, (((1,), (1,)), ((), ())), preferred_element_type=jnp.float32)
+
+    def near_tap(tap):
+        a, c = tap // 3 - 1, tap % 3 - 1
+        first, last = max(0, a * near_step), min(n, n + a * near_step)
+        if first >= last:
+            return
+        weight = tap_weight(tap)
+        to = first - a * near_step
+        if c == 0:
+            acc[to * rows : (to + last - first) * rows] += product(xc[first * rows : last * rows], weight)
+        else:
+            source, offset = (xl, skip) if c < 0 else (xh, 0)
+            result = product(source[first * side : last * side], weight)
+            for i in range((last - first) * deep):
+                base = to * rows + i * plane + offset
+                acc[base : base + edge] += result[i * edge : (i + 1) * edge]
+
+    def far_tap(tap):
+        a = tap - near_taps - 1
+        first, last = max(0, a * far_step), min(n, n + a * far_step)
+        if first >= last:
+            return
+        to = first - a * far_step
+        acc[to * rows : (to + last - first) * rows] += product(hc[first * rows : last * rows], tap_weight(tap))
+
+    def turn():
+        for i in range(n):
+            at = slice(i * rows, (i + 1) * rows)
+            keep = mf[at]
+            value = jnp.maximum(acc[at], 0.0) * jnp.concatenate([keep] * (channels // 128), axis=1)
+            split(value, hc, i * rows, rows)
+            acc[at] = xs[i]
+
+    def take_features():
+        for i in range(1, n):
+            d = (g + i) % n
+            arrival(xs, x_send, x_recv, d).wait_recv()
+            arrival(ms, m_send, m_recv, d).wait_recv()
+        flags = [ms[i] for i in range(n)]
+        flags.append(jnp.zeros((128 - n * 8, 128), jnp.float32))
+        flags = jnp.transpose(jnp.concatenate(flags, axis=0))
+        for i in range(n):
+            value = xs[i]
+            split(value, xc, i * rows, rows)
+            planes = [value[z * plane : (z + 1) * plane] for z in range(deep)]
+            split(jnp.concatenate([one[:edge] for one in planes], axis=0), xl, i * side, side)
+            split(jnp.concatenate([one[skip:] for one in planes], axis=0), xh, i * side, side)
+            for z in range(deep):
+                column = flags[:plane, i * 8 + z : i * 8 + z + 1]
+                mf[i * rows + z * plane : i * rows + (z + 1) * plane, :] = jnp.broadcast_to(column, (plane, 128))
+        acc[...] = jnp.zeros_like(acc)
+
+    def compute(grp):
+        if grp == 0:
+            take_features()
+        for tap in range(grp * GROUP, (grp + 1) * GROUP):
+            if tap == near_taps:
+                turn()
+            if tap < near_taps:
+                near_tap(tap)
+            else:
+                far_tap(tap)
+
+    for tau in range(groups + line + 1):
+        for t in range(line):
+            if 0 <= tau - t < groups:
+                line_stage(t, tau - t)
+        for t in range(line):
+            if 0 <= tau - 1 - t < groups:
+                pair_stage(t, tau - 1 - t)
+        if tau == 0:
+            for i in (2, 1, 3) if n == 4 else range(1, n):
+                d = (g + i) % n
+                exchange(feat, xs, x_send, x_recv, d).start()
+                exchange(mask, ms, m_send, m_recv, d).start()
+        grp = tau - line - 1
+        if 0 <= grp < groups:
+            for t in range(line):
+                core_stage(t, grp)
+            compute(grp)
+
+    for i in (2, 1, 3) if n == 4 else range(1, n):
+        d = (g + i) % n
+        at = pl.ds(pl.multiple_of(d * rows, rows), rows)
+        exchange(feat, xs, x_send, x_recv, d).wait_send()
+        stage[d] = acc[at] * jnp.concatenate([mf[at]] * (channels // 128), axis=1)
+        exchange(stage, out, r_send, r_recv, d).start()
+    at = pl.ds(pl.multiple_of(g * rows, rows), rows)
+    stage[g] = acc[at] * jnp.concatenate([mf[at]] * (channels // 128), axis=1)
+    own = pltpu.make_async_copy(stage.at[g], out.at[g], own_sem)
+    own.start()
+    for grp in range(groups):
+        for t in range(line):
+            finish(t, grp)
+    own.wait()
+    for i in range(1, n):
+        d = (g + i) % n
+        exchange(mask, ms, m_send, m_recv, d).wait_send()
+        exchange(stage, out, r_send, r_recv, d).wait_send()
+        arrival(out, r_send, r_recv, d).wait_recv()
+
+
+def fits(features, weight):
+    slab_z, slab_x, span_y, channels = features.shape
+    n, m = lax.axis_size("gz"), lax.axis_size("xy")
+    deep, plane, part = slab_z // n, span_y * slab_x, weight.shape[2]
+    return (
+        FAR_DILATION >= span_y > NEAR_DILATION
+        and NEAR_DILATION >= slab_x * m
+        and NEAR_DILATION % slab_z == 0 and FAR_DILATION % slab_z == 0
+        and n % 2 == 0 and m % 2 == 0 and m >= 4
+        and slab_z % n == 0 and deep <= 8 and n <= 16
+        and plane <= 128 and plane % 8 == 0 and NEAR_DILATION * slab_x % 8 == 0
+        and deep * plane % 16 == 0 and deep * (span_y - NEAR_DILATION) * slab_x % 16 == 0
+        and channels % 128 == 0 and part % 16 == 0 and part * m == channels
+    )
+
+
+def fast(features, block_mask, near_kernel_weight, far_kernel_weight):
+    slab_z, slab_x, span_y, channels = features.shape
+    n, m = lax.axis_size("gz"), lax.axis_size("xy")
+    part = near_kernel_weight.shape[2]
+    deep, plane = slab_z // n, span_y * slab_x
+    rows, side = deep * plane, deep * (span_y - NEAR_DILATION) * slab_x
+    near = jnp.swapaxes(near_kernel_weight, 1, 2)
+    far = jnp.swapaxes(far_kernel_weight, 1, 2)
+    active = jnp.repeat(jnp.repeat(jnp.repeat(block_mask, B, 0), B, 1), B, 2).astype(jnp.float32)
+    active = jnp.swapaxes(active, 1, 2)
+    feat = (active[..., None] * jnp.swapaxes(features, 1, 2)).reshape(n, rows, channels)
+    mask = jnp.pad(active.reshape(n, deep, plane), ((0, 0), (0, 8 - deep), (0, 128 - plane)))
+    taps = 12
+    groups, line = taps // GROUP, m // 2
+    dma = pltpu.SemaphoreType.DMA
+    vmem, hbm = pl.BlockSpec(memory_space=pltpu.VMEM), pl.BlockSpec(memory_space=pl.ANY)
+    out = pl.pallas_call(
+        functools.partial(section_kernel, n, deep, span_y, NEAR_DILATION // slab_z, FAR_DILATION // slab_z),
+        out_shape=jax.ShapeDtypeStruct((n, rows, channels), jnp.float32),
+        in_specs=[hbm, vmem, hbm, hbm],
+        out_specs=hbm,
+        scratch_shapes=[
+            pltpu.VMEM((taps, m * part, channels), jnp.float32),
+            pltpu.VMEM((n, rows, channels), jnp.float32),
+            pltpu.VMEM((n, rows, channels), jnp.float32),
+            pltpu.VMEM((n, 8, 128), jnp.float32),
+            pltpu.VMEM((n * rows, 128), jnp.float32),
+            pltpu.VMEM((n * rows, 3 * channels), jnp.bfloat16),
+            pltpu.VMEM((n * side, 3 * channels), jnp.bfloat16),
+            pltpu.VMEM((n * side, 3 * channels), jnp.bfloat16),
+            pltpu.VMEM((n * rows, channels), jnp.float32),
+            pltpu.VMEM((n * rows, 3 * channels), jnp.bfloat16),
+            dma((line, groups)), dma((line, groups)), dma((line, groups)), dma((m, groups)),
+            dma((line, groups)), dma((line, groups)), dma((m, groups)),
+            dma((n,)), dma((n,)), dma((n,)), dma((n,)), dma((n,)), dma((n,)), dma((7,)), dma,
+        ],
+        compiler_params=pltpu.CompilerParams(
+            collective_id=0, has_side_effects=True, vmem_limit_bytes=48 * 1024 * 1024),
+        cost_estimate=pl.CostEstimate(flops=3 * 10**9, bytes_accessed=4 * 10**6, transcendentals=0),
+    )(feat, mask, near, far)
+    return jnp.swapaxes(out.reshape(slab_z, span_y, slab_x, channels), 1, 2)
+
+
+def local(features, block_mask, near_kernel_weight, far_kernel_weight):
+    form = fast if fits(features, near_kernel_weight) else general
+    return form(features, block_mask, near_kernel_weight, far_kernel_weight)
+
+
 def solution(mesh):
     in_specs = (
         P("gz", "xy", None, None),

time: 129 us -> 53 us (0.41)
  the two profiles are of different devices: /device:TPU:2 before, /device:TPU:1 now
where the time goes in v2:
time: 53 us; the launch traced here: 52.4 us
  Pallas kernels  45.7 us (86%)
  local copies, waits for them, and re-layouts  4.91 us (9%)
  other arithmetic  1.73 us (3%)
    pallas_call x1, Pallas kernels, fast(): pl.pallas_call(functools.partial(section_kernel, n, deep, span_y, NEAR_DI...  45.7 us
    unnamed x6, local copies, waits for them, and re-layouts  2.38 us
    mul x1, other arithmetic, fast(): active[..., None] * jnp.swapaxes(features, 1, 2)  1.73 us
    reshape x1, local copies, waits for them, and re-layouts, fast(): return jnp.swapaxes(out.reshape(slab_z, span_y, slab_x, channels), 1, 2)  1.46 us

profile of v2, /device:TPU:1, one launch (start us, length us, event | category | flops | bytes accessed | tf_op | source)
XLA Modules:
  0.0 52.4 jit_solution(3906568664484999567)
XLA Ops:
  0.0 0.0 copy-start.2
  0.0 0.7 %copy-done.2 = s32[8,1,14]{2,1,0:T(1,128)S(1)} copy-done((s32[8,1,14]{2,1,0:T(1,128)S(1)}, s32[8,1,14]{2,1,0:T(1,128)}, u32[]{:S(2)}) %copy-start.2) | copy-done | bytes 472
  0.7 0.1 copy.11
  0.8 0.1 copy.12
  0.9 0.1 reshape.21
  1.0 0.1 copy.13
  1.1 1.7 %multiply_bitcast_fusion = f32[16,28,2,256]{3,2,1,0:T(2,128)S(1)} fusion(f32[16,2,28,256]{3,1,2,0:T(2,128)} %param.4, f32[16,28]{1,0:T(8,128)S(1)} %copy.12), kind=kLoop, calls=%fused_computation | loop fusion | flops 229376 | bytes 1836800 | tf_op jit(solution)/shard_map/mul | solution.py:401
  2.9 0.0 copy-start
  2.9 0.6 %reshape.20.feat = f32[4,224,256]{2,1,0:T(8,128)S(1)} reshape(f32[16,28,2,256]{3,2,1,0:T(2,128)S(1)} %multiply_bitcast_fusion) | data formatting | bytes 1835008 | tf_op jit(solution)/shard_map/reshape | solution.py:401
  3.5 0.5 copy-done
  4.1 0.0 copy-start.1
  4.1 1.2 %copy-done.1 = f32[27,256,32]{1,2,0:T(8,128)S(1)} copy-done((f32[27,256,32]{1,2,0:T(8,128)S(1)}, f32[27,256,32]{1,2,0:T(8,128)}, u32[]{:S(2)}) %copy-start.1) | copy-done | bytes 884760
  5.2 45.7 %shard_map.46 = f32[4,224,256]{2,1,0:T(8,128)S(1)} custom-call(f32[4,224,256]{2,1,0:T(8,128)S(1)} %reshape.20.feat, f32[4,8,128]{2,1,0:T(8,128)S(1)} %pad.4.mask, f32[27,32,256]{2,1,0:T(8,128)S(1)} %bitcast.13, f32[27,32,256]{2,1,0:T(8,128)S(1)} %bitcast.14), custom_call_target="tpu_custom_call" | custom-call | flops 3000000000 | bytes 4000000 | tf_op jit(solution)/shard_map/pallas_call | solution.py:407
  51.0 1.5 %reshape.22 = f32[16,28,2,256]{3,2,1,0:T(2,128)} reshape(f32[4,224,256]{2,1,0:T(8,128)S(1)} %shard_map.46) | data formatting | bytes 1835008 | tf_op jit(solution)/shard_map/reshape | solution.py:431
  (6 shorter events, 0.1 us)
Async XLA Ops:
  0.0 0.7 %copy-start.2 = (s32[8,1,14]{2,1,0:T(1,128)S(1)}, s32[8,1,14]{2,1,0:T(1,128)}, u32[]{:S(2)}) copy-start(s32[8,1,14]{2,1,0:T(1,128)} %param.5) | copy-start | bytes 1348
  2.9 1.2 %copy-start = (f32[27,256,32]{1,2,0:T(8,128)S(1)}, f32[27,256,32]{1,2,0:T(8,128)}, u32[]{:S(2)}) copy-start(f32[27,256,32]{1,2,0:T(8,128)} %param.6) | copy-start | bytes 2654212
  4.1 1.2 %copy-start.1 = (f32[27,256,32]{1,2,0:T(8,128)S(1)}, f32[27,256,32]{1,2,0:T(8,128)}, u32[]{:S(2)}) copy-start(f32[27,256,32]{1,2,0:T(8,128)} %param.7) | copy-start | bytes 2654212

commit v3 on v2

--- a/solution.py
+++ b/solution.py
@@ -11,7 +11,6 @@
 NEAR_DILATION = 16
 FAR_DILATION = 32
 MESH = pl.DeviceIdType.MESH
-GROUP = 2
 
 
 def offsets(dilation, extent):
@@ -86,8 +85,8 @@
 def section_kernel(
     n, deep, span_y, near_step, far_step,
     feat, mask, near, far, out,
-    wall, stage, xs, ms, mf, xc, xl, xh, acc, hc,
-    up_send, down_send, pair_send, core_send, line_recv, pair_recv, core_recv,
+    wall, raw, stage, xs, ms, mf, xc, xl, xh, acc, hc,
+    line_send, pair_send, core_send, line_recv, pair_recv, core_recv,
     x_send, x_recv, m_send, m_recv, r_send, r_recv, load_sem, own_sem,
 ):
     taps, wide, channels = wall.shape
@@ -95,7 +94,6 @@
     half = part // 2
     positions = wide // part
     line = positions // 2
-    groups = taps // GROUP
     rows = xs.shape[1]
     plane = rows // deep
     skip = plane * NEAR_DILATION // span_y
@@ -116,7 +114,7 @@
         loads.append((near.at[pl.ds(9 * a + 3, 3)], wall.at[pl.ds(3 * a, 3), home, :]))
     for a in range(3):
         loads.append((far.at[pl.ds(9 * a + 4, 1)], wall.at[pl.ds(near_taps + a, 1), home, :]))
-    loads.append((feat.at[g], xs.at[g]))
+    loads.append((feat, raw))
     loads = [pltpu.make_async_copy(a, b, load_sem.at[i]) for i, (a, b) in enumerate(loads)]
     for load in loads:
         load.start()
@@ -126,39 +124,28 @@
         pl.semaphore_signal(barrier, inc=1, device_id={"gz": (g + i) % n}, device_id_type=MESH)
     pl.semaphore_signal(barrier, inc=1, device_id={"xy": mate}, device_id_type=MESH)
 
-    @pl.when(pos > 0)
-    def _():
-        pl.semaphore_signal(barrier, inc=1, device_id={"xy": s - 2}, device_id_type=MESH)
-
-    @pl.when(pos < line - 1)
-    def _():
-        pl.semaphore_signal(barrier, inc=1, device_id={"xy": s + 2}, device_id_type=MESH)
+    for i in range(1, line):
+        pl.semaphore_signal(barrier, inc=1, device_id={"xy": 2 * ((pos + i) % line) + col}, device_id_type=MESH)
 
     ms[g] = mask[g]
-    for load in loads:
+    for load in loads[:-1]:
         load.wait()
-
-    @pl.when((pos > 0) & (pos < line - 1))
-    def _():
-        pl.semaphore_wait(barrier, n + 2)
-
-    @pl.when((pos == 0) | (pos == line - 1))
-    def _():
-        pl.semaphore_wait(barrier, n + 1)
+    pl.semaphore_wait(barrier, n + line - 1)
 
     def piece(p, q, h, grp):
         start = pl.multiple_of((2 * p + q) * part + h * half, half)
-        return wall.at[pl.ds(GROUP * grp, GROUP), pl.ds(start, half), :]
-
-    def up(p, grp):
+        return wall.at[tap_of(grp), pl.ds(start, half), :]
+
+    def along(k, grp):
+        ref = piece(pos, col, core, grp)
+        where = 2 * ((pos + k) % line) + col
+        return pltpu.make_async_remote_copy(
+            ref, ref, line_send.at[k, grp], line_recv.at[pos, grp], device_id={"xy": where}, device_id_type=MESH)
+
+    def from_line(p, grp):
         ref = piece(p, col, core, grp)
         return pltpu.make_async_remote_copy(
-            ref, ref, up_send.at[p, grp], line_recv.at[p, grp], device_id={"xy": s + 2}, device_id_type=MESH)
-
-    def down(p, grp):
-        ref = piece(p, col, core, grp)
-        return pltpu.make_async_remote_copy(
-            ref, ref, down_send.at[p, grp], line_recv.at[p, grp], device_id={"xy": s - 2}, device_id_type=MESH)
+            ref, ref, line_send.at[0, grp], line_recv.at[p, grp], device_id={"xy": 2 * p + col}, device_id_type=MESH)
 
     def across(p, q, grp):
         ref = piece(p, q, core, grp)
@@ -171,80 +158,38 @@
         return pltpu.make_async_remote_copy(
             ref, ref, core_send.at[where, grp], core_recv.at[where, grp], device_id={"gz": twin}, device_id_type=MESH)
 
-    def both(t, act):
-        @pl.when(pos - t >= 0)
-        def _():
-            act(pos - t)
-
-        if t > 0:
-            @pl.when(pos + t < line)
-            def _():
-                act(pos + t)
-
-    def line_stage(t, grp):
-        @pl.when(pos - t >= 0)
-        def _():
-            if t > 0:
-                up(pos - t, grp).wait_recv()
-
-            @pl.when(pos + 1 < line)
-            def _():
-                up(pos - t, grp).start()
-
-            across(pos - t, col, grp).start()
-            if t > 0:
-                to_twin(pos - t, col, core, grp).start()
-
-        @pl.when(pos + t < line)
-        def _():
-            if t > 0:
-                down(pos + t, grp).wait_recv()
-
-            @pl.when(pos >= 1)
-            def _():
-                down(pos + t, grp).start()
-
-            if t > 0:
-                across(pos + t, col, grp).start()
-                to_twin(pos + t, col, core, grp).start()
-
-    def pair_stage(t, grp):
-        def act(p):
+    others = [(pos + k) % line for k in range(1, line)]
+
+    def line_stage(grp):
+        for p in others:
+            from_line(p, grp).wait_recv()
+            across(p, col, grp).start()
+            to_twin(p, col, core, grp).start()
+
+    def pair_stage(grp):
+        for p in [pos] + others:
             across(p, 1 - col, grp).wait_recv()
             to_twin(p, 1 - col, core, grp).start()
 
-        both(t, act)
-
-    def core_stage(t, grp):
-        def act(p):
-            if t > 0:
-                to_twin(p, col, 1 - core, grp).wait_recv()
+    def core_stage(grp):
+        for p in others:
+            to_twin(p, col, 1 - core, grp).wait_recv()
+        for p in [pos] + others:
             to_twin(p, 1 - col, 1 - core, grp).wait_recv()
 
-        both(t, act)
-
-    def finish(t, grp):
-        @pl.when(pos - t >= 0)
-        def _():
-            @pl.when(pos + 1 < line)
-            def _():
-                up(pos - t, grp).wait_send()
-
-            across(pos - t, col, grp).wait_send()
-            to_twin(pos - t, 1 - col, core, grp).wait_send()
-            if t > 0:
-                to_twin(pos - t, col, core, grp).wait_send()
-
-        @pl.when(pos + t < line)
-        def _():
-            @pl.when(pos >= 1)
-            def _():
-                down(pos + t, grp).wait_send()
-
-            if t > 0:
-                across(pos + t, col, grp).wait_send()
-                to_twin(pos + t, 1 - col, core, grp).wait_send()
-                to_twin(pos + t, col, core, grp).wait_send()
+    def finish(grp):
+        for k in range(1, line):
+            along(k, grp).wait_send()
+        for p in [pos] + others:
+            across(p, col, grp).wait_send()
+            to_twin(p, 1 - col, core, grp).wait_send()
+        for p in others:
+            to_twin(p, col, core, grp).wait_send()
+
+    low = g < n // 2
+
+    def tap_of(grp):
+        return grp if grp < near_taps else jnp.where(low, grp, near_taps + taps - 1 - grp)
 
     def exchange(src, dst, send, recv, d):
         return pltpu.make_async_remote_copy(
@@ -270,6 +215,25 @@
 
     def product(lhs, weight):
         return lax.dot_general(lhs, weight, (((1,), (1,)), ((), ())), preferred_element_type=jnp.float32)
+
+    def spread(source, ref, i):
+        for z in range(deep):
+            column = source[:plane, i * 8 + z : i * 8 + z + 1]
+            ref[i * rows + z * plane : i * rows + (z + 1) * plane, :] = jnp.broadcast_to(column, (plane, 128))
+
+    def flags_of(ref):
+        flags = [ref[i] for i in range(n)]
+        flags.append(jnp.zeros((128 - n * 8, 128), jnp.float32))
+        return jnp.transpose(jnp.concatenate(flags, axis=0))
+
+    def keep(at):
+        return jnp.concatenate([mf[at]] * (channels // 128), axis=1)
+
+    def mask_features(d):
+        for z in range(deep):
+            value = raw[d * deep + z].reshape(plane, channels)
+            at = pl.ds(pl.multiple_of(d * rows + z * plane, 8), plane)
+            stage[d, z * plane : (z + 1) * plane] = value * keep(at)
 
     def near_tap(tap):
         a, c = tap // 3 - 1, tap % 3 - 1
@@ -295,11 +259,34 @@
         to = first - a * far_step
         acc[to * rows : (to + last - first) * rows] += product(hc[first * rows : last * rows], tap_weight(tap))
 
+    def give(i):
+        d = (g + i) % n
+        at = pl.ds(pl.multiple_of(d * rows, rows), rows)
+        exchange(stage, xs, x_send, x_recv, d).wait_send()
+        stage[d] = acc[at] * keep(at)
+        exchange(stage, out, r_send, r_recv, d).start()
+
+    def far_stage(grp):
+        order = grp - near_taps
+
+        @pl.when(low)
+        def _():
+            far_tap(near_taps + order)
+            if order == 1:
+                for d in range(n // 2, n):
+                    give(d - g)
+
+        @pl.when(jnp.logical_not(low))
+        def _():
+            far_tap(near_taps + 2 - order)
+            if order == 1:
+                for d in range(n // 2):
+                    give(d + n - g)
+
     def turn():
         for i in range(n):
             at = slice(i * rows, (i + 1) * rows)
-            keep = mf[at]
-            value = jnp.maximum(acc[at], 0.0) * jnp.concatenate([keep] * (channels // 128), axis=1)
+            value = jnp.maximum(acc[at], 0.0) * keep(at)
             split(value, hc, i * rows, rows)
             acc[at] = xs[i]
 
@@ -308,62 +295,61 @@
             d = (g + i) % n
             arrival(xs, x_send, x_recv, d).wait_recv()
             arrival(ms, m_send, m_recv, d).wait_recv()
-        flags = [ms[i] for i in range(n)]
-        flags.append(jnp.zeros((128 - n * 8, 128), jnp.float32))
-        flags = jnp.transpose(jnp.concatenate(flags, axis=0))
+        flags = flags_of(ms)
         for i in range(n):
             value = xs[i]
             split(value, xc, i * rows, rows)
             planes = [value[z * plane : (z + 1) * plane] for z in range(deep)]
             split(jnp.concatenate([one[:edge] for one in planes], axis=0), xl, i * side, side)
             split(jnp.concatenate([one[skip:] for one in planes], axis=0), xh, i * side, side)
-            for z in range(deep):
-                column = flags[:plane, i * 8 + z : i * 8 + z + 1]
-                mf[i * rows + z * plane : i * rows + (z + 1) * plane, :] = jnp.broadcast_to(column, (plane, 128))
+            spread(flags, mf, i)
         acc[...] = jnp.zeros_like(acc)
 
     def compute(grp):
         if grp == 0:
             take_features()
-        for tap in range(grp * GROUP, (grp + 1) * GROUP):
-            if tap == near_taps:
+        if grp < near_taps:
+            near_tap(grp)
+            if grp == near_taps - 1:
                 turn()
-            if tap < near_taps:
-                near_tap(tap)
-            else:
-                far_tap(tap)
-
-    for tau in range(groups + line + 1):
-        for t in range(line):
-            if 0 <= tau - t < groups:
-                line_stage(t, tau - t)
-        for t in range(line):
-            if 0 <= tau - 1 - t < groups:
-                pair_stage(t, tau - 1 - t)
-        if tau == 0:
-            for i in (2, 1, 3) if n == 4 else range(1, n):
-                d = (g + i) % n
-                exchange(feat, xs, x_send, x_recv, d).start()
-                exchange(mask, ms, m_send, m_recv, d).start()
-        grp = tau - line - 1
-        if 0 <= grp < groups:
-            for t in range(line):
-                core_stage(t, grp)
-            compute(grp)
-
-    for i in (2, 1, 3) if n == 4 else range(1, n):
+        else:
+            far_stage(grp)
+
+    for grp in range(taps):
+        for k in range(1, line):
+            along(k, grp).start()
+        across(pos, col, grp).start()
+    flags = flags_of(mask)
+    for i in range(n):
+        spread(flags, mf, i)
+    loads[-1].wait()
+    half_way = n // 2
+    near_by = [i for i in range(1, n) if i != half_way]
+    for i in [half_way] + near_by:
         d = (g + i) % n
-        at = pl.ds(pl.multiple_of(d * rows, rows), rows)
-        exchange(feat, xs, x_send, x_recv, d).wait_send()
-        stage[d] = acc[at] * jnp.concatenate([mf[at]] * (channels // 128), axis=1)
-        exchange(stage, out, r_send, r_recv, d).start()
+        mask_features(d)
+        exchange(stage, xs, x_send, x_recv, d).start()
+        exchange(mask, ms, m_send, m_recv, d).start()
+    mask_features(g)
+    xs[g] = stage[g]
+
+    for tau in range(taps + 2):
+        if tau < taps:
+            line_stage(tau)
+        if 0 <= tau - 1 < taps:
+            pair_stage(tau - 1)
+        if 0 <= tau - 2:
+            core_stage(tau - 2)
+            compute(tau - 2)
+
+    for i in range(1, n // 2):
+        give((g // (n // 2)) * (n // 2) + (g + i) % (n // 2) + n - g)
     at = pl.ds(pl.multiple_of(g * rows, rows), rows)
-    stage[g] = acc[at] * jnp.concatenate([mf[at]] * (channels // 128), axis=1)
+    stage[g] = acc[at] * keep(at)
     own = pltpu.make_async_copy(stage.at[g], out.at[g], own_sem)
     own.start()
-    for grp in range(groups):
-        for t in range(line):
-            finish(t, grp)
+    for grp in range(taps):
+        finish(grp)
     own.wait()
     for i in range(1, n):
         d = (g + i) % n
@@ -380,7 +366,7 @@
         FAR_DILATION >= span_y > NEAR_DILATION
         and NEAR_DILATION >= slab_x * m
         and NEAR_DILATION % slab_z == 0 and FAR_DILATION % slab_z == 0
-        and n % 2 == 0 and m % 2 == 0 and m >= 4
+        and n % 2 == 0 and 2 * FAR_DILATION >= n * slab_z and m % 2 == 0 and m >= 4
         and slab_z % n == 0 and deep <= 8 and n <= 16
         and plane <= 128 and plane % 8 == 0 and NEAR_DILATION * slab_x % 8 == 0
         and deep * plane % 16 == 0 and deep * (span_y - NEAR_DILATION) * slab_x % 16 == 0
@@ -398,10 +384,10 @@
     far = jnp.swapaxes(far_kernel_weight, 1, 2)
     active = jnp.repeat(jnp.repeat(jnp.repeat(block_mask, B, 0), B, 1), B, 2).astype(jnp.float32)
     active = jnp.swapaxes(active, 1, 2)
-    feat = (active[..., None] * jnp.swapaxes(features, 1, 2)).reshape(n, rows, channels)
+    feat = jnp.swapaxes(features, 1, 2)
     mask = jnp.pad(active.reshape(n, deep, plane), ((0, 0), (0, 8 - deep), (0, 128 - plane)))
     taps = 12
-    groups, line = taps // GROUP, m // 2
+    groups, line = taps, m // 2
     dma = pltpu.SemaphoreType.DMA
     vmem, hbm = pl.BlockSpec(memory_space=pltpu.VMEM), pl.BlockSpec(memory_space=pl.ANY)
     out = pl.pallas_call(
@@ -411,6 +397,7 @@
         out_specs=hbm,
         scratch_shapes=[
             pltpu.VMEM((taps, m * part, channels), jnp.float32),
+            pltpu.VMEM(feat.shape, jnp.float32),
             pltpu.VMEM((n, rows, channels), jnp.float32),
             pltpu.VMEM((n, rows, channels), jnp.float32),
             pltpu.VMEM((n, 8, 128), jnp.float32),
@@ -420,12 +407,12 @@
             pltpu.VMEM((n * side, 3 * channels), jnp.bfloat16),
             pltpu.VMEM((n * rows, channels), jnp.float32),
             pltpu.VMEM((n * rows, 3 * channels), jnp.bfloat16),
-            dma((line, groups)), dma((line, groups)), dma((line, groups)), dma((m, groups)),
+            dma((line, groups)), dma((line, groups)), dma((m, groups)),
             dma((line, groups)), dma((line, groups)), dma((m, groups)),
             dma((n,)), dma((n,)), dma((n,)), dma((n,)), dma((n,)), dma((n,)), dma((7,)), dma,
         ],
         compiler_params=pltpu.CompilerParams(
-            collective_id=0, has_side_effects=True, vmem_limit_bytes=48 * 1024 * 1024),
+            collective_id=0, has_side_effects=True, vmem_limit_bytes=60 * 1024 * 1024),
         cost_estimate=pl.CostEstimate(flops=3 * 10**9, bytes_accessed=4 * 10**6, transcendentals=0),
     )(feat, mask, near, far)
     return jnp.swapaxes(out.reshape(slab_z, span_y, slab_x, channels), 1, 2)

time: 53 us -> 54.7 us (1.032)
  Pallas kernels: 45.7 us -> 50.1 us
  other arithmetic: 1.73 us -> 0.01 us
  local copies, waits for them, and re-layouts: 4.91 us -> 4.31 us
    pallas_call x1, Pallas kernels: 45.7 us -> 50.1 us  [fast(): pl.pallas_call(functools.partial(section_kernel, n, deep, span_y, NEAR_DI...]
    mul x1 -> x0, other arithmetic: 1.73 us -> none  [fast(): active[..., None] * jnp.swapaxes(features, 1, 2)]
    unnamed x6 -> x2, local copies, waits for them, and re-layouts: 2.38 us -> 0.69 us
    reshape x1, local copies, waits for them, and re-layouts: 1.46 us -> 2.64 us  [fast(): return jnp.swapaxes(out.reshape(slab_z, span_y, slab_x, channels), 1, 2)]
    reshape x1 -> x0, local copies, waits for them, and re-layouts: 0.63 us -> none  [fast(): (active[..., None] * jnp.swapaxes(features, 1, 2)).reshape(n, rows, chann...]
    pad x1, local copies, waits for them, and re-layouts: 0.01 us -> 0.63 us  [fast(): jnp.pad(active.reshape(n, deep, plane), ((0, 0), (0, 8 - deep), (0, 128 -...]
where the time goes in v3:
time: 54.7 us; the launch traced here: 54.4 us
  Pallas kernels  50.1 us (92%)
  local copies, waits for them, and re-layouts  4.31 us (8%)
    pallas_call x1, Pallas kernels, fast(): pl.pallas_call(functools.partial(section_kernel, n, deep, span_y, NEAR_DI...  50.1 us
    reshape x1, local copies, waits for them, and re-layouts, fast(): return jnp.swapaxes(out.reshape(slab_z, span_y, slab_x, channels), 1, 2)  2.64 us

profile of v3, /device:TPU:1, one launch (start us, length us, event | category | flops | bytes accessed | tf_op | source)
XLA Modules:
  0.0 54.4 jit_solution(1150061427588033242)
XLA Ops:
  0.0 0.0 copy-start
  0.0 0.7 %copy-done = s32[8,1,14]{2,1,0:T(1,128)S(1)} copy-done((s32[8,1,14]{2,1,0:T(1,128)S(1)}, s32[8,1,14]{2,1,0:T(1,128)}, u32[]{:S(2)}) %copy-start) | copy-done | bytes 472
  0.7 0.1 copy.10
  0.8 0.1 reshape.17
  1.0 0.1 copy.11
  1.1 0.6 %pad.4.mask = f32[4,8,128]{2,1,0:T(8,128)} pad(f32[4,4,56]{2,1,0:T(4,128)S(1)} %copy.11, f32[]{:T(128)} %constant.2.clone.1), padding=0_0x0_4x0_72 | pad | bytes 19972 | tf_op jit(solution)/shard_map/jit(_pad)/pad | solution.py:388
  1.7 50.1 %shard_map.46 = f32[4,224,256]{2,1,0:T(8,128)} custom-call(f32[16,28,2,256]{3,2,1,0:T(2,128)} %bitcast.14, f32[4,8,128]{2,1,0:T(8,128)} %pad.4.mask, f32[27,32,256]{2,1,0:T(8,128)} %bitcast.15, f32[27,32,256]{2,1,0:T(8,128)} %bitcast.16), custom_call_target="tpu_custom_call" | custom-call | flops 3000000000 | bytes 4000000 | tf_op jit(solution)/shard_map/pallas_call | solution.py:393
  51.8 2.6 %reshape.18 = f32[16,28,2,256]{3,2,1,0:T(2,128)} reshape(f32[4,224,256]{2,1,0:T(8,128)} %shard_map.46) | data formatting | bytes 1835008 | tf_op jit(solution)/shard_map/reshape | solution.py:418
  (5 shorter events, 0.0 us)
Async XLA Ops:
  0.0 0.7 %copy-start = (s32[8,1,14]{2,1,0:T(1,128)S(1)}, s32[8,1,14]{2,1,0:T(1,128)}, u32[]{:S(2)}) copy-start(s32[8,1,14]{2,1,0:T(1,128)} %param.5) | copy-start | bytes 1348

commit v4 on v3

--- a/solution.py
+++ b/solution.py
@@ -10,6 +10,7 @@
 B = 2
 NEAR_DILATION = 16
 FAR_DILATION = 32
+WINDOW = 4
 MESH = pl.DeviceIdType.MESH
 
 
@@ -85,15 +86,12 @@
 def section_kernel(
     n, deep, span_y, near_step, far_step,
     feat, mask, near, far, out,
-    wall, raw, stage, xs, ms, mf, xc, xl, xh, acc, hc,
+    wall, raw, raw_mask, stage, back, xs, ms, mf, xc, xl, xh, acc, hc,
     line_send, pair_send, core_send, line_recv, pair_recv, core_recv,
-    x_send, x_recv, m_send, m_recv, r_send, r_recv, load_sem, own_sem,
+    x_send, x_recv, m_send, m_recv, r_send, r_recv, load_sem, out_sem,
 ):
-    taps, wide, channels = wall.shape
-    part = near.shape[1]
-    half = part // 2
-    positions = wide // part
-    line = positions // 2
+    taps, _, _, line, half, channels = wall.shape
+    slab_x = raw.shape[2]
     rows = xs.shape[1]
     plane = rows // deep
     skip = plane * NEAR_DILATION // span_y
@@ -108,13 +106,12 @@
     twin = g + 1 - 2 * core
     mate = s + 1 - 2 * col
 
-    home = pl.ds(pl.multiple_of(s * part, part), part)
-    loads = []
+    loads = [(mask, raw_mask), (feat, raw)]
+    rows_of = pl.ds(pl.multiple_of(core * half, half), half)
     for a in range(3):
-        loads.append((near.at[pl.ds(9 * a + 3, 3)], wall.at[pl.ds(3 * a, 3), home, :]))
+        loads.append((near.at[pl.ds(9 * a + 3, 3), rows_of], wall.at[pl.ds(3 * a, 3), core, col, pos]))
     for a in range(3):
-        loads.append((far.at[pl.ds(9 * a + 4, 1)], wall.at[pl.ds(near_taps + a, 1), home, :]))
-    loads.append((feat, raw))
+        loads.append((far.at[9 * a + 4, rows_of], wall.at[near_taps + a, core, col, pos]))
     loads = [pltpu.make_async_copy(a, b, load_sem.at[i]) for i, (a, b) in enumerate(loads)]
     for load in loads:
         load.start()
@@ -127,64 +124,52 @@
     for i in range(1, line):
         pl.semaphore_signal(barrier, inc=1, device_id={"xy": 2 * ((pos + i) % line) + col}, device_id_type=MESH)
 
-    ms[g] = mask[g]
-    for load in loads[:-1]:
+    for load in loads[2:]:
         load.wait()
     pl.semaphore_wait(barrier, n + line - 1)
 
-    def piece(p, q, h, grp):
-        start = pl.multiple_of((2 * p + q) * part + h * half, half)
-        return wall.at[tap_of(grp), pl.ds(start, half), :]
-
     def along(k, grp):
-        ref = piece(pos, col, core, grp)
+        ref = wall.at[tap_of(grp), core, col, pos]
         where = 2 * ((pos + k) % line) + col
         return pltpu.make_async_remote_copy(
             ref, ref, line_send.at[k, grp], line_recv.at[pos, grp], device_id={"xy": where}, device_id_type=MESH)
 
     def from_line(p, grp):
-        ref = piece(p, col, core, grp)
+        ref = wall.at[tap_of(grp), core, col, p]
         return pltpu.make_async_remote_copy(
             ref, ref, line_send.at[0, grp], line_recv.at[p, grp], device_id={"xy": 2 * p + col}, device_id_type=MESH)
 
-    def across(p, q, grp):
-        ref = piece(p, q, core, grp)
-        return pltpu.make_async_remote_copy(
-            ref, ref, pair_send.at[p, grp], pair_recv.at[p, grp], device_id={"xy": mate}, device_id_type=MESH)
-
-    def to_twin(p, q, h, grp):
-        ref = piece(p, q, h, grp)
-        where = 2 * p + q
-        return pltpu.make_async_remote_copy(
-            ref, ref, core_send.at[where, grp], core_recv.at[where, grp], device_id={"gz": twin}, device_id_type=MESH)
-
-    others = [(pos + k) % line for k in range(1, line)]
+    def across(q, grp):
+        ref = wall.at[tap_of(grp), core, q]
+        return pltpu.make_async_remote_copy(
+            ref, ref, pair_send.at[grp], pair_recv.at[grp], device_id={"xy": mate}, device_id_type=MESH)
+
+    def to_twin(h, grp):
+        ref = wall.at[tap_of(grp), h]
+        return pltpu.make_async_remote_copy(
+            ref, ref, core_send.at[grp], core_recv.at[grp], device_id={"gz": twin}, device_id_type=MESH)
+
+    def line_start(grp):
+        for k in range(1, line):
+            along(k, grp).start()
 
     def line_stage(grp):
-        for p in others:
-            from_line(p, grp).wait_recv()
-            across(p, col, grp).start()
-            to_twin(p, col, core, grp).start()
+        for k in range(1, line):
+            from_line((pos + k) % line, grp).wait_recv()
+        across(col, grp).start()
 
     def pair_stage(grp):
-        for p in [pos] + others:
-            across(p, 1 - col, grp).wait_recv()
-            to_twin(p, 1 - col, core, grp).start()
+        across(1 - col, grp).wait_recv()
+        to_twin(core, grp).start()
 
     def core_stage(grp):
-        for p in others:
-            to_twin(p, col, 1 - core, grp).wait_recv()
-        for p in [pos] + others:
-            to_twin(p, 1 - col, 1 - core, grp).wait_recv()
+        to_twin(1 - core, grp).wait_recv()
 
     def finish(grp):
         for k in range(1, line):
             along(k, grp).wait_send()
-        for p in [pos] + others:
-            across(p, col, grp).wait_send()
-            to_twin(p, 1 - col, core, grp).wait_send()
-        for p in others:
-            to_twin(p, col, core, grp).wait_send()
+        across(col, grp).wait_send()
+        to_twin(core, grp).wait_send()
 
     low = g < n // 2
 
@@ -194,6 +179,10 @@
     def exchange(src, dst, send, recv, d):
         return pltpu.make_async_remote_copy(
             src.at[d], dst.at[g], send.at[d], recv.at[g], device_id={"gz": d}, device_id_type=MESH)
+
+    def toward(d):
+        return pltpu.make_async_remote_copy(
+            ms.at[g], ms.at[g], m_send.at[d], m_recv.at[g], device_id={"gz": d}, device_id_type=MESH)
 
     def arrival(dst, send, recv, d):
         return pltpu.make_async_remote_copy(
@@ -208,7 +197,7 @@
         ref[at, 2 * channels :] = high
 
     def tap_weight(tap):
-        value = wall[tap]
+        value = jnp.concatenate([wall[tap, h, q, p] for p in range(line) for q in range(2) for h in range(2)], axis=0)
         high = value.astype(jnp.bfloat16)
         low = (value - high.astype(jnp.float32)).astype(jnp.bfloat16)
         return jnp.concatenate([high, high, low], axis=1)
@@ -216,15 +205,19 @@
     def product(lhs, weight):
         return lax.dot_general(lhs, weight, (((1,), (1,)), ((), ())), preferred_element_type=jnp.float32)
 
-    def spread(source, ref, i):
+    def columns(ref, picks):
+        chosen = [ref[slab, pl.ds(row, 1), :] for slab, row in picks]
+        chosen.append(jnp.zeros((-len(picks) % 8 + 8, 128), jnp.float32))
+        r = lax.broadcasted_iota(jnp.int32, (plane, 128), 0)
+        k = lax.broadcasted_iota(jnp.int32, (plane, 128), 1)
+        block = (r % slab_x) // B * (span_y // B) + r // slab_x // B
+        return product((block == k).astype(jnp.float32), jnp.concatenate(chosen, axis=0))
+
+    def spread(flags, i):
         for z in range(deep):
-            column = source[:plane, i * 8 + z : i * 8 + z + 1]
-            ref[i * rows + z * plane : i * rows + (z + 1) * plane, :] = jnp.broadcast_to(column, (plane, 128))
-
-    def flags_of(ref):
-        flags = [ref[i] for i in range(n)]
-        flags.append(jnp.zeros((128 - n * 8, 128), jnp.float32))
-        return jnp.transpose(jnp.concatenate(flags, axis=0))
+            at = i * (deep // B) + z // B
+            column = flags[:, at : at + 1]
+            mf[i * rows + z * plane : i * rows + (z + 1) * plane, :] = jnp.broadcast_to(column, (plane, 128))
 
     def keep(at):
         return jnp.concatenate([mf[at]] * (channels // 128), axis=1)
@@ -264,7 +257,7 @@
         at = pl.ds(pl.multiple_of(d * rows, rows), rows)
         exchange(stage, xs, x_send, x_recv, d).wait_send()
         stage[d] = acc[at] * keep(at)
-        exchange(stage, out, r_send, r_recv, d).start()
+        exchange(stage, back, r_send, r_recv, d).start()
 
     def far_stage(grp):
         order = grp - near_taps
@@ -295,14 +288,14 @@
             d = (g + i) % n
             arrival(xs, x_send, x_recv, d).wait_recv()
             arrival(ms, m_send, m_recv, d).wait_recv()
-        flags = flags_of(ms)
+        flags = columns(ms, [(i, g * (deep // B) + j) for i in range(n) for j in range(deep // B)])
         for i in range(n):
             value = xs[i]
             split(value, xc, i * rows, rows)
             planes = [value[z * plane : (z + 1) * plane] for z in range(deep)]
             split(jnp.concatenate([one[:edge] for one in planes], axis=0), xl, i * side, side)
             split(jnp.concatenate([one[skip:] for one in planes], axis=0), xh, i * side, side)
-            spread(flags, mf, i)
+            spread(flags, i)
         acc[...] = jnp.zeros_like(acc)
 
     def compute(grp):
@@ -315,27 +308,32 @@
         else:
             far_stage(grp)
 
-    for grp in range(taps):
-        for k in range(1, line):
-            along(k, grp).start()
-        across(pos, col, grp).start()
-    flags = flags_of(mask)
+    for grp in range(WINDOW):
+        line_start(grp)
+    for load in loads[:2]:
+        load.wait()
+    ms[g] = jnp.zeros((ms.shape[1], 128), jnp.float32)
+    for x in range(raw_mask.shape[1]):
+        value = raw_mask[:, x, :].astype(jnp.float32)
+        ms[g, :, x * (span_y // B) : (x + 1) * (span_y // B)] = value
+    flags = columns(ms, [(g, j) for j in range(n * deep // B)])
     for i in range(n):
-        spread(flags, mf, i)
-    loads[-1].wait()
+        spread(flags, i)
     half_way = n // 2
     near_by = [i for i in range(1, n) if i != half_way]
     for i in [half_way] + near_by:
         d = (g + i) % n
         mask_features(d)
         exchange(stage, xs, x_send, x_recv, d).start()
-        exchange(mask, ms, m_send, m_recv, d).start()
+        toward(d).start()
     mask_features(g)
     xs[g] = stage[g]
 
     for tau in range(taps + 2):
         if tau < taps:
             line_stage(tau)
+            if tau + WINDOW < taps:
+                line_start(tau + WINDOW)
         if 0 <= tau - 1 < taps:
             pair_stage(tau - 1)
         if 0 <= tau - 2:
@@ -344,18 +342,25 @@
 
     for i in range(1, n // 2):
         give((g // (n // 2)) * (n // 2) + (g + i) % (n // 2) + n - g)
+    def deliver(d, source):
+        for z in range(deep):
+            raw[d * deep + z] = source[z * plane : (z + 1) * plane].reshape(raw.shape[1:])
+        return pltpu.make_async_copy(raw.at[pl.ds(d * deep, deep)], out.at[pl.ds(d * deep, deep)], out_sem.at[d])
+
     at = pl.ds(pl.multiple_of(g * rows, rows), rows)
-    stage[g] = acc[at] * keep(at)
-    own = pltpu.make_async_copy(stage.at[g], out.at[g], own_sem)
-    own.start()
+    deliver(g, acc[at] * keep(at)).start()
     for grp in range(taps):
         finish(grp)
-    own.wait()
     for i in range(1, n):
         d = (g + i) % n
-        exchange(mask, ms, m_send, m_recv, d).wait_send()
-        exchange(stage, out, r_send, r_recv, d).wait_send()
-        arrival(out, r_send, r_recv, d).wait_recv()
+        toward(d).wait_send()
+        exchange(stage, back, r_send, r_recv, d).wait_send()
+    for i in near_by + [half_way]:
+        d = (g + i) % n
+        arrival(back, r_send, r_recv, d).wait_recv()
+        deliver(d, back[d]).start()
+    for d in range(n):
+        pltpu.make_async_copy(raw.at[pl.ds(d * deep, deep)], out.at[pl.ds(d * deep, deep)], out_sem.at[d]).wait()
 
 
 def fits(features, weight):
@@ -366,8 +371,8 @@
         FAR_DILATION >= span_y > NEAR_DILATION
         and NEAR_DILATION >= slab_x * m
         and NEAR_DILATION % slab_z == 0 and FAR_DILATION % slab_z == 0
-        and n % 2 == 0 and 2 * FAR_DILATION >= n * slab_z and m % 2 == 0 and m >= 4
-        and slab_z % n == 0 and deep <= 8 and n <= 16
+        and n % 4 == 0 and 2 * FAR_DILATION >= n * slab_z and m % 2 == 0 and m >= 4
+        and slab_z % (B * n) == 0 and slab_x % B == 0 and span_y % B == 0 and slab_z // B % 8 == 0
         and plane <= 128 and plane % 8 == 0 and NEAR_DILATION * slab_x % 8 == 0
         and deep * plane % 16 == 0 and deep * (span_y - NEAR_DILATION) * slab_x % 16 == 0
         and channels % 128 == 0 and part % 16 == 0 and part * m == channels
@@ -382,40 +387,39 @@
     rows, side = deep * plane, deep * (span_y - NEAR_DILATION) * slab_x
     near = jnp.swapaxes(near_kernel_weight, 1, 2)
     far = jnp.swapaxes(far_kernel_weight, 1, 2)
-    active = jnp.repeat(jnp.repeat(jnp.repeat(block_mask, B, 0), B, 1), B, 2).astype(jnp.float32)
-    active = jnp.swapaxes(active, 1, 2)
     feat = jnp.swapaxes(features, 1, 2)
-    mask = jnp.pad(active.reshape(n, deep, plane), ((0, 0), (0, 8 - deep), (0, 128 - plane)))
     taps = 12
-    groups, line = taps, m // 2
+    line = m // 2
     dma = pltpu.SemaphoreType.DMA
-    vmem, hbm = pl.BlockSpec(memory_space=pltpu.VMEM), pl.BlockSpec(memory_space=pl.ANY)
+    hbm = pl.BlockSpec(memory_space=pl.ANY)
     out = pl.pallas_call(
         functools.partial(section_kernel, n, deep, span_y, NEAR_DILATION // slab_z, FAR_DILATION // slab_z),
-        out_shape=jax.ShapeDtypeStruct((n, rows, channels), jnp.float32),
-        in_specs=[hbm, vmem, hbm, hbm],
+        out_shape=jax.ShapeDtypeStruct(feat.shape, jnp.float32),
+        in_specs=[hbm] * 4,
         out_specs=hbm,
         scratch_shapes=[
-            pltpu.VMEM((taps, m * part, channels), jnp.float32),
+            pltpu.VMEM((taps, 2, 2, line, part // 2, channels), jnp.float32),
             pltpu.VMEM(feat.shape, jnp.float32),
+            pltpu.VMEM(block_mask.shape, jnp.int32),
             pltpu.VMEM((n, rows, channels), jnp.float32),
             pltpu.VMEM((n, rows, channels), jnp.float32),
-            pltpu.VMEM((n, 8, 128), jnp.float32),
+            pltpu.VMEM((n, rows, channels), jnp.float32),
+            pltpu.VMEM((n, slab_z // B, 128), jnp.float32),
             pltpu.VMEM((n * rows, 128), jnp.float32),
             pltpu.VMEM((n * rows, 3 * channels), jnp.bfloat16),
             pltpu.VMEM((n * side, 3 * channels), jnp.bfloat16),
             pltpu.VMEM((n * side, 3 * channels), jnp.bfloat16),
             pltpu.VMEM((n * rows, channels), jnp.float32),
             pltpu.VMEM((n * rows, 3 * channels), jnp.bfloat16),
-            dma((line, groups)), dma((line, groups)), dma((m, groups)),
-            dma((line, groups)), dma((line, groups)), dma((m, groups)),
-            dma((n,)), dma((n,)), dma((n,)), dma((n,)), dma((n,)), dma((n,)), dma((7,)), dma,
+            dma((line, taps)), dma((taps,)), dma((taps,)),
+            dma((line, taps)), dma((taps,)), dma((taps,)),
+            dma((n,)), dma((n,)), dma((n,)), dma((n,)), dma((n,)), dma((n,)), dma((8,)), dma((n,)),
         ],
         compiler_params=pltpu.CompilerParams(
             collective_id=0, has_side_effects=True, vmem_limit_bytes=60 * 1024 * 1024),
         cost_estimate=pl.CostEstimate(flops=3 * 10**9, bytes_accessed=4 * 10**6, transcendentals=0),
-    )(feat, mask, near, far)
-    return jnp.swapaxes(out.reshape(slab_z, span_y, slab_x, channels), 1, 2)
+    )(feat, block_mask, near, far)
+    return jnp.swapaxes(out, 1, 2)
 
 
 def local(features, block_mask, near_kernel_weight, far_kernel_weight):

time: 54.7 us -> 51.9 us (0.949)
  local copies, waits for them, and re-layouts: 4.31 us -> 2.42 us
  Pallas kernels: 50.1 us -> 49.3 us
    reshape x3 -> x0, local copies, waits for them, and re-layouts: 2.86 us -> none  [the longest x1 2.64 us: fast(): return jnp.swapaxes(out.reshape(slab_z, span_y, slab_x, channels), 1, 2)]
    unnamed x2 -> x1, local copies, waits for them, and re-layouts: 0.69 us -> 2.42 us
    pallas_call x1, Pallas kernels: 50.1 us -> 49.3 us  [fast(): pl.pallas_call(functools.partial(section_kernel, n, deep, span_y, NEAR_DI...]
    pad x1 -> x0, local copies, waits for them, and re-layouts: 0.63 us -> none  [fast(): jnp.pad(active.reshape(n, deep, plane), ((0, 0), (0, 8 - deep), (0, 128 -...]
where the time goes in v4:
time: 51.9 us; the launch traced here: 51.7 us
  Pallas kernels  49.3 us (95%)
  local copies, waits for them, and re-layouts  2.42 us (5%)
    pallas_call x1, Pallas kernels, fast(): pl.pallas_call(functools.partial(section_kernel, n, deep, span_y, NEAR_DI...  49.3 us
    unnamed x1, local copies, waits for them, and re-layouts  2.42 us

profile of v4, /device:TPU:1, one launch (start us, length us, event | category | flops | bytes accessed | tf_op | source)
XLA Modules:
  0.0 51.7 jit_solution(5659588211762949910)
XLA Ops:
  0.0 49.3 %shard_map.46 = f32[16,28,2,256]{3,2,1,0:T(2,128)} custom-call(f32[16,28,2,256]{3,2,1,0:T(2,128)} %bitcast.5, s32[8,1,14]{2,1,0:T(1,128)} %mask.1, f32[27,32,256]{2,1,0:T(8,128)} %bitcast.6, f32[27,32,256]{2,1,0:T(8,128)} %bitcast.7), custom_call_target="tpu_custom_call" | custom-call | flops 3000000000 | bytes 4000000 | tf_op jit(solution)/shard_map/pallas_call | solution.py:395
  49.3 2.4 %copy.6 = f32[16,2,28,256]{3,1,2,0:T(2,128)} copy(f32[16,2,28,256]{3,1,2,0:T(2,128)} %bitcast.4) | data formatting | bytes 1835008

commit v5 on v4

--- a/solution.py
+++ b/solution.py
@@ -11,6 +11,7 @@
 NEAR_DILATION = 16
 FAR_DILATION = 32
 WINDOW = 4
+LEAD = 9
 MESH = pl.DeviceIdType.MESH
 
 
@@ -86,7 +87,7 @@
 def section_kernel(
     n, deep, span_y, near_step, far_step,
     feat, mask, near, far, out,
-    wall, raw, raw_mask, stage, back, xs, ms, mf, xc, xl, xh, acc, hc,
+    wall, raw, raw_mask, stage, back, xs, ms, mf, xc, xl, xh, acc, hc, total,
     line_send, pair_send, core_send, line_recv, pair_recv, core_recv,
     x_send, x_recv, m_send, m_recv, r_send, r_recv, load_sem, out_sem,
 ):
@@ -174,7 +175,7 @@
     low = g < n // 2
 
     def tap_of(grp):
-        return grp if grp < near_taps else jnp.where(low, grp, near_taps + taps - 1 - grp)
+        return jnp.where(low | (grp < near_taps), grp, near_taps + taps - 1 - grp)
 
     def exchange(src, dst, send, recv, d):
         return pltpu.make_async_remote_copy(
@@ -191,7 +192,7 @@
     def split(value, ref, start, count):
         high = value.astype(jnp.bfloat16)
         low = (value - high.astype(jnp.float32)).astype(jnp.bfloat16)
-        at = pl.ds(start, count)
+        at = pl.ds(pl.multiple_of(start, 16), count)
         ref[at, 0:channels] = high
         ref[at, channels : 2 * channels] = low
         ref[at, 2 * channels :] = high
@@ -228,85 +229,80 @@
             at = pl.ds(pl.multiple_of(d * rows + z * plane, 8), plane)
             stage[d, z * plane : (z + 1) * plane] = value * keep(at)
 
-    def near_tap(tap):
-        a, c = tap // 3 - 1, tap % 3 - 1
-        first, last = max(0, a * near_step), min(n, n + a * near_step)
-        if first >= last:
+    def slab(i):
+        return pl.ds(pl.multiple_of(i * rows, rows), rows)
+
+    def near_tap(a, c):
+        weight = tap_weight(3 * a + c)
+        base = pl.multiple_of((2 - a) * near_step * rows, rows)
+        if c == 1:
+            at = pl.ds(base, n * rows)
+            acc[at] += product(xc[...], weight)
             return
-        weight = tap_weight(tap)
-        to = first - a * near_step
-        if c == 0:
-            acc[to * rows : (to + last - first) * rows] += product(xc[first * rows : last * rows], weight)
-        else:
-            source, offset = (xl, skip) if c < 0 else (xh, 0)
-            result = product(source[first * side : last * side], weight)
-            for i in range((last - first) * deep):
-                base = to * rows + i * plane + offset
-                acc[base : base + edge] += result[i * edge : (i + 1) * edge]
-
-    def far_tap(tap):
-        a = tap - near_taps - 1
-        first, last = max(0, a * far_step), min(n, n + a * far_step)
-        if first >= last:
+        source, offset = (xl, skip) if c == 0 else (xh, 0)
+        result = product(source[...], weight)
+        for i in range(n * deep):
+            at = pl.ds(pl.multiple_of(base + i * plane + offset, 8), edge)
+            acc[at] += result[i * edge : (i + 1) * edge]
+
+    def give(d):
+        exchange(stage, xs, x_send, x_recv, d).wait_send()
+        stage[d] = total[slab(d)] * keep(slab(d))
+        exchange(stage, back, r_send, r_recv, d).start()
+
+    def far_stage(order):
+        weight = tap_weight(tap_of(near_taps + order))
+        if order == 1:
+            total[...] += product(hc[...], weight)
             return
-        to = first - a * far_step
-        acc[to * rows : (to + last - first) * rows] += product(hc[first * rows : last * rows], tap_weight(tap))
-
-    def give(i):
-        d = (g + i) % n
-        at = pl.ds(pl.multiple_of(d * rows, rows), rows)
-        exchange(stage, xs, x_send, x_recv, d).wait_send()
-        stage[d] = acc[at] * keep(at)
-        exchange(stage, back, r_send, r_recv, d).start()
-
-    def far_stage(grp):
-        order = grp - near_taps
-
-        @pl.when(low)
+        count = (n - far_step) * rows
+        front = low if order == 0 else jnp.logical_not(low)
+        source = pl.multiple_of(jnp.where(front, 0, far_step * rows), rows)
+        target = pl.multiple_of(jnp.where(front, far_step * rows, 0), rows)
+        total[pl.ds(target, count)] += product(hc[pl.ds(source, count)], weight)
+
+    def turn(i, _):
+        at = slab(i)
+        value = jnp.maximum(acc[pl.ds(pl.multiple_of((i + near_step) * rows, rows), rows)], 0.0) * keep(at)
+        split(value, hc, i * rows, rows)
+        total[at] = xs[i]
+        return 0
+
+    def take_slab(i, _):
+        value = xs[i]
+        split(value, xc, i * rows, rows)
+        planes = [value[z * plane : (z + 1) * plane] for z in range(deep)]
+        split(jnp.concatenate([one[:edge] for one in planes], axis=0), xl, i * side, side)
+        split(jnp.concatenate([one[skip:] for one in planes], axis=0), xh, i * side, side)
+        return 0
+
+    def step(tau):
+        @pl.when(tau < taps)
         def _():
-            far_tap(near_taps + order)
-            if order == 1:
-                for d in range(n // 2, n):
-                    give(d - g)
-
-        @pl.when(jnp.logical_not(low))
+            line_stage(tau)
+
+        @pl.when(tau + WINDOW < taps)
         def _():
-            far_tap(near_taps + 2 - order)
-            if order == 1:
-                for d in range(n // 2):
-                    give(d + n - g)
-
-    def turn():
-        for i in range(n):
-            at = slice(i * rows, (i + 1) * rows)
-            value = jnp.maximum(acc[at], 0.0) * keep(at)
-            split(value, hc, i * rows, rows)
-            acc[at] = xs[i]
-
-    def take_features():
-        for i in range(1, n):
-            d = (g + i) % n
-            arrival(xs, x_send, x_recv, d).wait_recv()
-            arrival(ms, m_send, m_recv, d).wait_recv()
-        flags = columns(ms, [(i, g * (deep // B) + j) for i in range(n) for j in range(deep // B)])
-        for i in range(n):
-            value = xs[i]
-            split(value, xc, i * rows, rows)
-            planes = [value[z * plane : (z + 1) * plane] for z in range(deep)]
-            split(jnp.concatenate([one[:edge] for one in planes], axis=0), xl, i * side, side)
-            split(jnp.concatenate([one[skip:] for one in planes], axis=0), xh, i * side, side)
-            spread(flags, i)
-        acc[...] = jnp.zeros_like(acc)
-
-    def compute(grp):
-        if grp == 0:
-            take_features()
-        if grp < near_taps:
-            near_tap(grp)
-            if grp == near_taps - 1:
-                turn()
-        else:
-            far_stage(grp)
+            line_start(tau + WINDOW)
+
+        @pl.when((tau >= 1) & (tau <= taps))
+        def _():
+            pair_stage(tau - 1)
+
+    def finish_all(grp, _):
+        finish(grp)
+        return 0
+
+    def lead(tau, _):
+        step(tau)
+        return 0
+
+    def near_row(a, _):
+        for c in range(3):
+            step(3 * a + c + LEAD)
+            core_stage(3 * a + c)
+            near_tap(a, c)
+        return 0
 
     for grp in range(WINDOW):
         line_start(grp)
@@ -319,44 +315,50 @@
     flags = columns(ms, [(g, j) for j in range(n * deep // B)])
     for i in range(n):
         spread(flags, i)
-    half_way = n // 2
-    near_by = [i for i in range(1, n) if i != half_way]
-    for i in [half_way] + near_by:
+    for k in range(n):
+        d = (g + n // 2 + k) % n
+        mask_features(d)
+        if k == n // 2:
+            xs[g] = stage[g]
+        else:
+            exchange(stage, xs, x_send, x_recv, d).start()
+            toward(d).start()
+
+    lax.fori_loop(0, LEAD, lead, 0)
+    acc[...] = jnp.zeros_like(acc)
+    for i in range(1, n):
         d = (g + i) % n
-        mask_features(d)
-        exchange(stage, xs, x_send, x_recv, d).start()
-        toward(d).start()
-    mask_features(g)
-    xs[g] = stage[g]
-
-    for tau in range(taps + 2):
-        if tau < taps:
-            line_stage(tau)
-            if tau + WINDOW < taps:
-                line_start(tau + WINDOW)
-        if 0 <= tau - 1 < taps:
-            pair_stage(tau - 1)
-        if 0 <= tau - 2:
-            core_stage(tau - 2)
-            compute(tau - 2)
-
+        arrival(xs, x_send, x_recv, d).wait_recv()
+        arrival(ms, m_send, m_recv, d).wait_recv()
+    flags = columns(ms, [(i, g * (deep // B) + j) for i in range(n) for j in range(deep // B)])
+    for i in range(n):
+        spread(flags, i)
+    lax.fori_loop(0, n, take_slab, 0)
+    lax.fori_loop(0, 3, near_row, 0)
+    lax.fori_loop(0, n, turn, 0)
+    for order in range(3):
+        step(near_taps + order + LEAD)
+        core_stage(near_taps + order)
+        far_stage(order)
+        if order == 1:
+            for i in range(n // 2):
+                give(jnp.where(low, n // 2, 0) + i)
     for i in range(1, n // 2):
-        give((g // (n // 2)) * (n // 2) + (g + i) % (n // 2) + n - g)
+        give(g // (n // 2) * (n // 2) + (g + i) % (n // 2))
+
     def deliver(d, source):
         for z in range(deep):
             raw[d * deep + z] = source[z * plane : (z + 1) * plane].reshape(raw.shape[1:])
         return pltpu.make_async_copy(raw.at[pl.ds(d * deep, deep)], out.at[pl.ds(d * deep, deep)], out_sem.at[d])
 
-    at = pl.ds(pl.multiple_of(g * rows, rows), rows)
-    deliver(g, acc[at] * keep(at)).start()
-    for grp in range(taps):
-        finish(grp)
+    deliver(g, total[slab(g)] * keep(slab(g))).start()
+    lax.fori_loop(0, taps, finish_all, 0)
     for i in range(1, n):
         d = (g + i) % n
         toward(d).wait_send()
         exchange(stage, back, r_send, r_recv, d).wait_send()
-    for i in near_by + [half_way]:
-        d = (g + i) % n
+    for k in list(range(n // 2 + 1, n)) + list(range(n // 2)):
+        d = (g + n // 2 + k) % n
         arrival(back, r_send, r_recv, d).wait_recv()
         deliver(d, back[d]).start()
     for d in range(n):
@@ -370,7 +372,7 @@
     return (
         FAR_DILATION >= span_y > NEAR_DILATION
         and NEAR_DILATION >= slab_x * m
-        and NEAR_DILATION % slab_z == 0 and FAR_DILATION % slab_z == 0
+        and NEAR_DILATION % slab_z == 0 and FAR_DILATION % slab_z == 0 and NEAR_DILATION < n * slab_z and FAR_DILATION < n * slab_z
         and n % 4 == 0 and 2 * FAR_DILATION >= n * slab_z and m % 2 == 0 and m >= 4
         and slab_z % (B * n) == 0 and slab_x % B == 0 and span_y % B == 0 and slab_z // B % 8 == 0
         and plane <= 128 and plane % 8 == 0 and NEAR_DILATION * slab_x % 8 == 0
@@ -409,8 +411,9 @@
             pltpu.VMEM((n * rows, 3 * channels), jnp.bfloat16),
             pltpu.VMEM((n * side, 3 * channels), jnp.bfloat16),
             pltpu.VMEM((n * side, 3 * channels), jnp.bfloat16),
+            pltpu.VMEM(((n + 2 * (NEAR_DILATION // slab_z)) * rows, channels), jnp.float32),
+            pltpu.VMEM((n * rows, 3 * channels), jnp.bfloat16),
             pltpu.VMEM((n * rows, channels), jnp.float32),
-            pltpu.VMEM((n * rows, 3 * channels), jnp.bfloat16),
             dma((line, taps)), dma((taps,)), dma((taps,)),
             dma((line, taps)), dma((taps,)), dma((taps,)),
             dma((n,)), dma((n,)), dma((n,)), dma((n,)), dma((n,)), dma((n,)), dma((8,)), dma((n,)),

time: 51.9 us -> 51 us (0.983)
  Pallas kernels: 49.3 us -> 48.3 us
    pallas_call x1, Pallas kernels: 49.3 us -> 48.3 us  [fast(): pl.pallas_call(functools.partial(section_kernel, n, deep, span_y, NEAR_DI...]
where the time goes in v5:
time: 51 us; the launch traced here: 50.8 us
  Pallas kernels  48.3 us (95%)
  local copies, waits for them, and re-layouts  2.42 us (5%)
    pallas_call x1, Pallas kernels, fast(): pl.pallas_call(functools.partial(section_kernel, n, deep, span_y, NEAR_DI...  48.3 us
    unnamed x1, local copies, waits for them, and re-layouts  2.42 us

profile of v5, /device:TPU:1, one launch (start us, length us, event | category | flops | bytes accessed | tf_op | source)
XLA Modules:
  0.0 50.8 jit_solution(8429246313915788372)
XLA Ops:
  0.0 48.3 %shard_map.46 = f32[16,28,2,256]{3,2,1,0:T(2,128)} custom-call(f32[16,28,2,256]{3,2,1,0:T(2,128)} %bitcast.5, s32[8,1,14]{2,1,0:T(1,128)} %mask.1, f32[27,32,256]{2,1,0:T(8,128)} %bitcast.6, f32[27,32,256]{2,1,0:T(8,128)} %bitcast.7), custom_call_target="tpu_custom_call" | custom-call | flops 3000000000 | bytes 4000000 | tf_op jit(solution)/shard_map/pallas_call | solution.py:397
  48.3 2.4 %copy.6 = f32[16,2,28,256]{3,1,2,0:T(2,128)} copy(f32[16,2,28,256]{3,1,2,0:T(2,128)} %bitcast.4) | data formatting | bytes 1835008

commit v6 on v5

--- a/solution.py
+++ b/solution.py
@@ -87,7 +87,7 @@
 def section_kernel(
     n, deep, span_y, near_step, far_step,
     feat, mask, near, far, out,
-    wall, raw, raw_mask, stage, back, xs, ms, mf, xc, xl, xh, acc, hc, total,
+    wall, ready, raw, raw_mask, stage, xs, ms, mf, xc, xl, xh, acc, hc, total,
     line_send, pair_send, core_send, line_recv, pair_recv, core_recv,
     x_send, x_recv, m_send, m_recv, r_send, r_recv, load_sem, out_sem,
 ):
@@ -197,14 +197,19 @@
         ref[at, channels : 2 * channels] = low
         ref[at, 2 * channels :] = high
 
-    def tap_weight(tap):
+    def prepare(grp):
+        core_stage(grp)
+        tap = tap_of(grp)
         value = jnp.concatenate([wall[tap, h, q, p] for p in range(line) for q in range(2) for h in range(2)], axis=0)
+        value = jnp.transpose(value)
         high = value.astype(jnp.bfloat16)
         low = (value - high.astype(jnp.float32)).astype(jnp.bfloat16)
-        return jnp.concatenate([high, high, low], axis=1)
+        ready[grp, 0:channels] = high
+        ready[grp, channels : 2 * channels] = high
+        ready[grp, 2 * channels :] = low
 
     def product(lhs, weight):
-        return lax.dot_general(lhs, weight, (((1,), (1,)), ((), ())), preferred_element_type=jnp.float32)
+        return jnp.dot(lhs, weight, preferred_element_type=jnp.float32)
 
     def columns(ref, picks):
         chosen = [ref[slab, pl.ds(row, 1), :] for slab, row in picks]
@@ -212,7 +217,8 @@
         r = lax.broadcasted_iota(jnp.int32, (plane, 128), 0)
         k = lax.broadcasted_iota(jnp.int32, (plane, 128), 1)
         block = (r % slab_x) // B * (span_y // B) + r // slab_x // B
-        return product((block == k).astype(jnp.float32), jnp.concatenate(chosen, axis=0))
+        spots, chosen = (block == k).astype(jnp.float32), jnp.concatenate(chosen, axis=0)
+        return lax.dot_general(spots, chosen, (((1,), (1,)), ((), ())), preferred_element_type=jnp.float32)
 
     def spread(flags, i):
         for z in range(deep):
@@ -233,7 +239,7 @@
         return pl.ds(pl.multiple_of(i * rows, rows), rows)
 
     def near_tap(a, c):
-        weight = tap_weight(3 * a + c)
+        weight = ready[3 * a + c]
         base = pl.multiple_of((2 - a) * near_step * rows, rows)
         if c == 1:
             at = pl.ds(base, n * rows)
@@ -248,10 +254,10 @@
     def give(d):
         exchange(stage, xs, x_send, x_recv, d).wait_send()
         stage[d] = total[slab(d)] * keep(slab(d))
-        exchange(stage, back, r_send, r_recv, d).start()
+        exchange(stage, out, r_send, r_recv, d).start()
 
     def far_stage(order):
-        weight = tap_weight(tap_of(near_taps + order))
+        weight = ready[near_taps + order]
         if order == 1:
             total[...] += product(hc[...], weight)
             return
@@ -289,6 +295,10 @@
         def _():
             pair_stage(tau - 1)
 
+        @pl.when((tau >= 2) & (tau <= taps + 1))
+        def _():
+            prepare(tau - 2)
+
     def finish_all(grp, _):
         finish(grp)
         return 0
@@ -299,9 +309,8 @@
 
     def near_row(a, _):
         for c in range(3):
+            near_tap(a, c)
             step(3 * a + c + LEAD)
-            core_stage(3 * a + c)
-            near_tap(a, c)
         return 0
 
     for grp in range(WINDOW):
@@ -337,8 +346,6 @@
     lax.fori_loop(0, 3, near_row, 0)
     lax.fori_loop(0, n, turn, 0)
     for order in range(3):
-        step(near_taps + order + LEAD)
-        core_stage(near_taps + order)
         far_stage(order)
         if order == 1:
             for i in range(n // 2):
@@ -346,23 +353,16 @@
     for i in range(1, n // 2):
         give(g // (n // 2) * (n // 2) + (g + i) % (n // 2))
 
-    def deliver(d, source):
-        for z in range(deep):
-            raw[d * deep + z] = source[z * plane : (z + 1) * plane].reshape(raw.shape[1:])
-        return pltpu.make_async_copy(raw.at[pl.ds(d * deep, deep)], out.at[pl.ds(d * deep, deep)], out_sem.at[d])
-
-    deliver(g, total[slab(g)] * keep(slab(g))).start()
+    stage[g] = total[slab(g)] * keep(slab(g))
+    own = pltpu.make_async_copy(stage.at[g], out.at[g], out_sem)
+    own.start()
     lax.fori_loop(0, taps, finish_all, 0)
     for i in range(1, n):
         d = (g + i) % n
         toward(d).wait_send()
-        exchange(stage, back, r_send, r_recv, d).wait_send()
-    for k in list(range(n // 2 + 1, n)) + list(range(n // 2)):
-        d = (g + n // 2 + k) % n
-        arrival(back, r_send, r_recv, d).wait_recv()
-        deliver(d, back[d]).start()
-    for d in range(n):
-        pltpu.make_async_copy(raw.at[pl.ds(d * deep, deep)], out.at[pl.ds(d * deep, deep)], out_sem.at[d]).wait()
+        exchange(stage, out, r_send, r_recv, d).wait_send()
+        arrival(out, r_send, r_recv, d).wait_recv()
+    own.wait()
 
 
 def fits(features, weight):
@@ -393,17 +393,16 @@
     taps = 12
     line = m // 2
     dma = pltpu.SemaphoreType.DMA
-    hbm = pl.BlockSpec(memory_space=pl.ANY)
     out = pl.pallas_call(
         functools.partial(section_kernel, n, deep, span_y, NEAR_DILATION // slab_z, FAR_DILATION // slab_z),
-        out_shape=jax.ShapeDtypeStruct(feat.shape, jnp.float32),
-        in_specs=[hbm] * 4,
-        out_specs=hbm,
+        out_shape=jax.ShapeDtypeStruct((n, rows, channels), jnp.float32),
+        in_specs=[pl.BlockSpec(memory_space=pltpu.HBM)] * 4,
+        out_specs=pl.BlockSpec(memory_space=pl.ANY),
         scratch_shapes=[
             pltpu.VMEM((taps, 2, 2, line, part // 2, channels), jnp.float32),
+            pltpu.VMEM((taps, 3 * channels, m * part), jnp.bfloat16),
             pltpu.VMEM(feat.shape, jnp.float32),
             pltpu.VMEM(block_mask.shape, jnp.int32),
-            pltpu.VMEM((n, rows, channels), jnp.float32),
             pltpu.VMEM((n, rows, channels), jnp.float32),
             pltpu.VMEM((n, rows, channels), jnp.float32),
             pltpu.VMEM((n, slab_z // B, 128), jnp.float32),
@@ -416,13 +415,13 @@
             pltpu.VMEM((n * rows, channels), jnp.float32),
             dma((line, taps)), dma((taps,)), dma((taps,)),
             dma((line, taps)), dma((taps,)), dma((taps,)),
-            dma((n,)), dma((n,)), dma((n,)), dma((n,)), dma((n,)), dma((n,)), dma((8,)), dma((n,)),
+            dma((n,)), dma((n,)), dma((n,)), dma((n,)), dma((n,)), dma((n,)), dma((8,)), dma,
         ],
         compiler_params=pltpu.CompilerParams(
             collective_id=0, has_side_effects=True, vmem_limit_bytes=60 * 1024 * 1024),
         cost_estimate=pl.CostEstimate(flops=3 * 10**9, bytes_accessed=4 * 10**6, transcendentals=0),
     )(feat, block_mask, near, far)
-    return jnp.swapaxes(out, 1, 2)
+    return jnp.swapaxes(out.reshape(feat.shape), 1, 2)
 
 
 def local(features, block_mask, near_kernel_weight, far_kernel_weight):

time: 51 us -> 54.7 us (1.073)
  Pallas kernels: 48.3 us -> 51.8 us
    pallas_call x1, Pallas kernels: 48.3 us -> 51.8 us  [fast(): pl.pallas_call(functools.partial(section_kernel, n, deep, span_y, NEAR_DI...]
    reshape x0 -> x1, local copies, waits for them, and re-layouts: none -> 2.64 us  [fast(): return jnp.swapaxes(out.reshape(feat.shape), 1, 2)]
    unnamed x1 -> x0, local copies, waits for them, and re-layouts: 2.42 us -> none
where the time goes in v6:
time: 54.7 us; the launch traced here: 54.5 us
  Pallas kernels  51.8 us (95%)
  local copies, waits for them, and re-layouts  2.64 us (5%)
    pallas_call x1, Pallas kernels, fast(): pl.pallas_call(functools.partial(section_kernel, n, deep, span_y, NEAR_DI...  51.8 us
    reshape x1, local copies, waits for them, and re-layouts, fast(): return jnp.swapaxes(out.reshape(feat.shape), 1, 2)  2.64 us

profile of v6, /device:TPU:1, one launch (start us, length us, event | category | flops | bytes accessed | tf_op | source)
XLA Modules:
  0.0 54.5 jit_solution(5213090135469784496)
XLA Ops:
  0.0 51.8 %shard_map.46 = f32[4,224,256]{2,1,0:T(8,128)} custom-call(f32[16,28,2,256]{3,2,1,0:T(2,128)} %bitcast.4, s32[8,1,14]{2,1,0:T(1,128)} %mask.1, f32[27,32,256]{2,1,0:T(8,128)} %bitcast.5, f32[27,32,256]{2,1,0:T(8,128)} %bitcast.6), custom_call_target="tpu_custom_call" | custom-call | flops 3000000000 | bytes 4000000 | tf_op jit(solution)/shard_map/pallas_call | solution.py:396
  51.8 2.6 %reshape.3 = f32[16,28,2,256]{3,2,1,0:T(2,128)} reshape(f32[4,224,256]{2,1,0:T(8,128)} %shard_map.46) | data formatting | bytes 1835008 | tf_op jit(solution)/shard_map/reshape | solution.py:424

commit v7 on v6

--- a/solution.py
+++ b/solution.py
@@ -12,6 +12,7 @@
 FAR_DILATION = 32
 WINDOW = 4
 LEAD = 9
+LAG = 3
 MESH = pl.DeviceIdType.MESH
 
 
@@ -291,13 +292,9 @@
         def _():
             line_start(tau + WINDOW)
 
-        @pl.when((tau >= 1) & (tau <= taps))
+        @pl.when((tau >= LAG) & (tau < taps + LAG))
         def _():
-            pair_stage(tau - 1)
-
-        @pl.when((tau >= 2) & (tau <= taps + 1))
-        def _():
-            prepare(tau - 2)
+            pair_stage(tau - LAG)
 
     def finish_all(grp, _):
         finish(grp)
@@ -305,12 +302,23 @@
 
     def lead(tau, _):
         step(tau)
+
+        @pl.when(tau >= 2 * LAG)
+        def _():
+            prepare(tau - 2 * LAG)
+
         return 0
 
     def near_row(a, _):
         for c in range(3):
+            tap = 3 * a + c
             near_tap(a, c)
-            step(3 * a + c + LEAD)
+            step(tap + LEAD)
+
+            @pl.when(tap + LEAD - 2 * LAG <= near_taps)
+            def _():
+                prepare(tap + LEAD - 2 * LAG)
+
         return 0
 
     for grp in range(WINDOW):
@@ -350,6 +358,8 @@
         if order == 1:
             for i in range(n // 2):
                 give(jnp.where(low, n // 2, 0) + i)
+        if order < 2:
+            prepare(near_taps + order + 1)
     for i in range(1, n // 2):
         give(g // (n // 2) * (n // 2) + (g + i) % (n // 2))
 

time: 54.7 us -> 46.8 us (0.86)
  Pallas kernels: 51.8 us -> 44 us
    pallas_call x1, Pallas kernels: 51.8 us -> 44 us  [fast(): pl.pallas_call(functools.partial(section_kernel, n, deep, span_y, NEAR_DI...]
where the time goes in v7:
time: 46.8 us; the launch traced here: 46.6 us
  Pallas kernels  44 us (94%)
  local copies, waits for them, and re-layouts  2.64 us (6%)
    pallas_call x1, Pallas kernels, fast(): pl.pallas_call(functools.partial(section_kernel, n, deep, span_y, NEAR_DI...  44 us
    reshape x1, local copies, waits for them, and re-layouts, fast(): return jnp.swapaxes(out.reshape(feat.shape), 1, 2)  2.64 us

profile of v7, /device:TPU:1, one launch (start us, length us, event | category | flops | bytes accessed | tf_op | source)
XLA Modules:
  0.0 46.6 jit_solution(8774564787241250372)
XLA Ops:
  0.0 44.0 %shard_map.46 = f32[4,224,256]{2,1,0:T(8,128)} custom-call(f32[16,28,2,256]{3,2,1,0:T(2,128)} %bitcast.4, s32[8,1,14]{2,1,0:T(1,128)} %mask.1, f32[27,32,256]{2,1,0:T(8,128)} %bitcast.5, f32[27,32,256]{2,1,0:T(8,128)} %bitcast.6), custom_call_target="tpu_custom_call" | custom-call | flops 3000000000 | bytes 4000000 | tf_op jit(solution)/shard_map/pallas_call | solution.py:406
  44.0 2.6 %reshape.3 = f32[16,28,2,256]{3,2,1,0:T(2,128)} reshape(f32[4,224,256]{2,1,0:T(8,128)} %shard_map.46) | data formatting | bytes 1835008 | tf_op jit(solution)/shard_map/reshape | solution.py:434

commit v8 on v7

--- a/solution.py
+++ b/solution.py
@@ -10,7 +10,7 @@
 B = 2
 NEAR_DILATION = 16
 FAR_DILATION = 32
-WINDOW = 4
+WINDOW = 6
 LEAD = 9
 LAG = 3
 MESH = pl.DeviceIdType.MESH
@@ -373,6 +373,13 @@
         exchange(stage, out, r_send, r_recv, d).wait_send()
         arrival(out, r_send, r_recv, d).wait_recv()
     own.wait()
+
+
+def unfold_kernel(rows, cells):
+    deep, span_y, slab_x, channels = cells.shape
+    plane = span_y * slab_x
+    for z in range(deep):
+        cells[z] = rows[0, z * plane : (z + 1) * plane].reshape(span_y, slab_x, channels)
 
 
 def fits(features, weight):
@@ -431,7 +438,14 @@
             collective_id=0, has_side_effects=True, vmem_limit_bytes=60 * 1024 * 1024),
         cost_estimate=pl.CostEstimate(flops=3 * 10**9, bytes_accessed=4 * 10**6, transcendentals=0),
     )(feat, block_mask, near, far)
-    return jnp.swapaxes(out.reshape(feat.shape), 1, 2)
+    cells = pl.pallas_call(
+        unfold_kernel,
+        out_shape=jax.ShapeDtypeStruct(feat.shape, jnp.float32),
+        grid=(n,),
+        in_specs=[pl.BlockSpec((1, rows, channels), lambda i: (i, 0, 0))],
+        out_specs=pl.BlockSpec((deep, span_y, slab_x, channels), lambda i: (i, 0, 0, 0)),
+    )(out)
+    return jnp.swapaxes(cells, 1, 2)
 
 
 def local(features, block_mask, near_kernel_weight, far_kernel_weight):

time: 46.8 us -> 48.7 us (1.041)
  Pallas kernels: 44 us -> 48.5 us
  local copies, waits for them, and re-layouts: 2.64 us -> 0 us
    pallas_call x0 -> x1, Pallas kernels: none -> 3.37 us  [fast(): pl.pallas_call(unfold_kernel, out_shape=jax.ShapeDtypeStruct(feat.shape,...]
    reshape x1 -> x0, local copies, waits for them, and re-layouts: 2.64 us -> none  [fast(): return jnp.swapaxes(out.reshape(feat.shape), 1, 2)]
    pallas_call x1, Pallas kernels: 44 us -> 45.1 us  [fast(): pl.pallas_call(functools.partial(section_kernel, n, deep, span_y, NEAR_DI...]
where the time goes in v8:
time: 48.7 us; the launch traced here: 48.5 us
  Pallas kernels  48.5 us (100%)
    pallas_call x1, Pallas kernels, fast(): pl.pallas_call(functools.partial(section_kernel, n, deep, span_y, NEAR_DI...  45.1 us
    pallas_call x1, Pallas kernels, fast(): pl.pallas_call(unfold_kernel, out_shape=jax.ShapeDtypeStruct(feat.shape,...  3.37 us

profile of v8, /device:TPU:1, one launch (start us, length us, event | category | flops | bytes accessed | tf_op | source)
XLA Modules:
  0.0 48.5 jit_solution(4443348518153479870)
XLA Ops:
  0.0 45.1 %shard_map.46.rows = f32[4,224,256]{2,1,0:T(8,128)} custom-call(f32[16,28,2,256]{3,2,1,0:T(2,128)} %bitcast.4, s32[8,1,14]{2,1,0:T(1,128)} %mask.1, f32[27,32,256]{2,1,0:T(8,128)} %bitcast.5, f32[27,32,256]{2,1,0:T(8,128)} %bitcast.6), custom_call_target="tpu_custom_call" | custom-call | flops 3000000000 | bytes 4000000 | tf_op jit(solution)/shard_map/pallas_call | solution.py:413
  45.1 3.4 %shard_map.47 = f32[16,28,2,256]{3,2,1,0:T(2,128)} custom-call(f32[4,224,256]{2,1,0:T(8,128)} %shard_map.46.rows), custom_call_target="tpu_custom_call" | custom-call | tf_op jit(solution)/shard_map/pallas_call | solution.py:441

commit v9 on v7

--- a/solution.py
+++ b/solution.py
@@ -10,7 +10,7 @@
 B = 2
 NEAR_DILATION = 16
 FAR_DILATION = 32
-WINDOW = 4
+WINDOW = 3
 LEAD = 9
 LAG = 3
 MESH = pl.DeviceIdType.MESH

time: 46.8 us -> 46.6 us (level)
  no operation moved by 1% of the time
where the time goes in v9:
time: 46.6 us; the launch traced here: 46.4 us
  Pallas kernels  43.8 us (94%)
  local copies, waits for them, and re-layouts  2.64 us (6%)
    pallas_call x1, Pallas kernels, fast(): pl.pallas_call(functools.partial(section_kernel, n, deep, span_y, NEAR_DI...  43.8 us
    reshape x1, local copies, waits for them, and re-layouts, fast(): return jnp.swapaxes(out.reshape(feat.shape), 1, 2)  2.64 us

profile of v9, /device:TPU:1, one launch (start us, length us, event | category | flops | bytes accessed | tf_op | source)
XLA Modules:
  0.0 46.4 jit_solution(14578035849912038391)
XLA Ops:
  0.0 43.8 %shard_map.46 = f32[4,224,256]{2,1,0:T(8,128)} custom-call(f32[16,28,2,256]{3,2,1,0:T(2,128)} %bitcast.4, s32[8,1,14]{2,1,0:T(1,128)} %mask.1, f32[27,32,256]{2,1,0:T(8,128)} %bitcast.5, f32[27,32,256]{2,1,0:T(8,128)} %bitcast.6), custom_call_target="tpu_custom_call" | custom-call | flops 3000000000 | bytes 4000000 | tf_op jit(solution)/shard_map/pallas_call | solution.py:406
  43.8 2.6 %reshape.3 = f32[16,28,2,256]{3,2,1,0:T(2,128)} reshape(f32[4,224,256]{2,1,0:T(8,128)} %shard_map.46) | data formatting | bytes 1835008 | tf_op jit(solution)/shard_map/reshape | solution.py:434

commit v10 on v9

--- a/solution.py
+++ b/solution.py
@@ -12,7 +12,7 @@
 FAR_DILATION = 32
 WINDOW = 3
 LEAD = 9
-LAG = 3
+LAG = 4
 MESH = pl.DeviceIdType.MESH
 
 

time: 46.6 us -> 45.5 us (0.976)
  Pallas kernels: 43.8 us -> 42.7 us
    pallas_call x1, Pallas kernels: 43.8 us -> 42.7 us  [fast(): pl.pallas_call(functools.partial(section_kernel, n, deep, span_y, NEAR_DI...]
where the time goes in v10:
time: 45.5 us; the launch traced here: 45.3 us
  Pallas kernels  42.7 us (94%)
  local copies, waits for them, and re-layouts  2.64 us (6%)
    pallas_call x1, Pallas kernels, fast(): pl.pallas_call(functools.partial(section_kernel, n, deep, span_y, NEAR_DI...  42.7 us
    reshape x1, local copies, waits for them, and re-layouts, fast(): return jnp.swapaxes(out.reshape(feat.shape), 1, 2)  2.64 us

profile of v10, /device:TPU:1, one launch (start us, length us, event | category | flops | bytes accessed | tf_op | source)
XLA Modules:
  0.0 45.3 jit_solution(11682206539658224499)
XLA Ops:
  0.0 42.7 %shard_map.46 = f32[4,224,256]{2,1,0:T(8,128)} custom-call(f32[16,28,2,256]{3,2,1,0:T(2,128)} %bitcast.4, s32[8,1,14]{2,1,0:T(1,128)} %mask.1, f32[27,32,256]{2,1,0:T(8,128)} %bitcast.5, f32[27,32,256]{2,1,0:T(8,128)} %bitcast.6), custom_call_target="tpu_custom_call" | custom-call | flops 3000000000 | bytes 4000000 | tf_op jit(solution)/shard_map/pallas_call | solution.py:406
  42.7 2.6 %reshape.3 = f32[16,28,2,256]{3,2,1,0:T(2,128)} reshape(f32[4,224,256]{2,1,0:T(8,128)} %shard_map.46) | data formatting | bytes 1835008 | tf_op jit(solution)/shard_map/reshape | solution.py:434
